TPU v7x, 32 devices: a whole 2x2x4 slice. The times are simulated.
32 devices in a mesh: seq: 8 (over z, x), head: 2 (over y), batch: 2 (over core).
Axes of the slice: x: 2, y: 2, z: 4, core: 2. Of those that a mesh axis runs over, the one named last changes fastest.
Arguments:
- query_states: bfloat16 [4096, 1024], P(('batch', 'seq'), 'head'), parts along dimension 0, may hold values from -8 to 8
- key_states: bfloat16 [4096, 1024], P(('batch', 'seq'), 'head'), parts along dimension 0, may hold values from -8 to 8
- value_states: bfloat16 [4096, 1024], P(('batch', 'seq'), 'head'), parts along dimension 0, may hold values from -6 to 6
- out_grad: bfloat16 [4096, 1024], P(('batch', 'seq'), 'head'), parts along dimension 0, may hold values from -192 to 192
- head_offsets: int32 [8], P('head'), may hold values from 0 to 2047
Outputs:
- query_grad: bfloat16 [4096, 1024], P(('batch', 'seq'), 'head'), parts along dimension 0
- key_grad: bfloat16 [4096, 1024], P(('batch', 'seq'), 'head'), parts along dimension 0
- value_grad: bfloat16 [4096, 1024], P(('batch', 'seq'), 'head'), parts along dimension 0
There are 2 independent parts, one for each index of `batch`. A program takes and returns all parts, laid end to end along the dimension named above; an argument that names none is the same for every part. Nothing has to cross between parts.
All inputs are finite; a program needn't handle non-finite values.
Results may differ from a plain program's by a relative error of at most 0.0056.
Values may be sent and summed in bfloat16 or wider, within the bound.
A program may use at most 128 MiB of HBM per device.

v0:
```python
import jax
import jax.numpy as jnp
from jax import lax
from jax.sharding import PartitionSpec as P

WINDOW = 1024


masked_score = -1e30


def from_partner(block, axis, apart):
    count = lax.axis_size(axis)
    route = []
    for low in range(count):
        high = low | 1 << apart
        if high != low and high < count:
            route += [(low, high), (high, low)]
    return lax.ppermute(block, axis, route)


def passed_along(value, axis, steps):
    count = lax.axis_size(axis)
    leading, last = (max(0, -steps), min(count, count - steps))
    return lax.ppermute(value, axis, [(source, source + steps) for source in range(leading, last)])


def forward_part(queries, keys_in, values_in, allowed, softmax_scale):
    scores = (
        jnp.einsum("qhd,khd->hqk", queries, keys_in, preferred_element_type=jnp.float32)
        * softmax_scale
    )
    scores = jnp.where(allowed[None], scores, masked_score)
    row_max = jnp.max(scores, axis=-1)
    weights = jnp.exp(scores - row_max[..., None])
    row_sum = jnp.sum(weights, axis=-1)
    row_out = jnp.einsum(
        "hqk,khd->qhd", weights.astype(jnp.bfloat16), values_in, preferred_element_type=jnp.float32
    )
    return (row_max.T, row_sum.T, row_out)


def backward_part(queries, keys_in, values_in, grads, allowed, log_norm, grad_dot, softmax_scale):
    scores = (
        jnp.einsum("qhd,khd->hqk", queries, keys_in, preferred_element_type=jnp.float32)
        * softmax_scale
    )
    scores = jnp.where(allowed[None], scores, masked_score)
    weights = jnp.exp(scores - log_norm.T[..., None])
    grad_values = jnp.einsum(
        "hqk,qhd->khd", weights.astype(jnp.bfloat16), grads, preferred_element_type=jnp.float32
    )
    grad_probs = jnp.einsum("qhd,khd->hqk", grads, values_in, preferred_element_type=jnp.float32)
    grad_scores = (weights * (grad_probs - grad_dot.T[..., None])).astype(jnp.bfloat16)
    grad_queries = (
        jnp.einsum("hqk,khd->qhd", grad_scores, keys_in, preferred_element_type=jnp.float32)
        * softmax_scale
    )
    grad_keys = (
        jnp.einsum("hqk,qhd->khd", grad_scores, queries, preferred_element_type=jnp.float32)
        * softmax_scale
    )
    return (grad_queries, grad_keys, grad_values)


def merge_stats(first_stats, second_stats):
    row_max = jnp.maximum(first_stats[0], second_stats[0])
    first_factor = jnp.exp(first_stats[0] - row_max)
    second_factor = jnp.exp(second_stats[0] - row_max)
    row_sum = first_stats[1] * first_factor + second_stats[1] * second_factor
    row_out = first_stats[2] * first_factor[..., None] + second_stats[2] * second_factor[..., None]
    return (row_max, row_sum, row_out)


def row_mask(source, chosen):
    return chosen.reshape((1,) + chosen.shape + (1,) * (source.ndim - 2))


def pick_rows(source, chosen):
    stride = chosen.shape[0]
    shaped = source.reshape((source.shape[0] // stride, stride) + source.shape[1:])
    return jnp.sum(jnp.where(row_mask(source, chosen), shaped, jnp.zeros((), source.dtype)), axis=1)


def put_rows(source, chosen, update):
    stride = chosen.shape[0]
    shaped = source.reshape((source.shape[0] // stride, stride) + source.shape[1:])
    return jnp.where(row_mask(source, chosen), update[:, None], shaped).reshape(source.shape)


def add_rows(source, chosen, update):
    stride = chosen.shape[0]
    shaped = source.reshape((source.shape[0] // stride, stride) + source.shape[1:])
    return (shaped + jnp.where(row_mask(source, chosen), update[:, None], 0.0)).reshape(
        source.shape
    )


def gather_pairs(group_pair, level_num, position):
    for bit_index in range(level_num):
        partner = from_partner(group_pair, "seq", bit_index)
        upper_half = position >> bit_index & 1 == 1
        group_pair = jnp.where(
            upper_half,
            jnp.concatenate([partner, group_pair], axis=1),
            jnp.concatenate([group_pair, partner], axis=1),
        )
    return group_pair


def block_view(grad_pair, level_num):
    blocks = 2**level_num
    return grad_pair.reshape((2, blocks, grad_pair.shape[1] // blocks) + grad_pair.shape[2:])


def halve_blocks(shaped, bit_index, position):
    paired = shaped.reshape((2, shaped.shape[1] // 2, 2) + shaped.shape[2:])
    upper_half = position >> bit_index & 1 == 1
    kept_half = jnp.where(upper_half, paired[:, :, 1], paired[:, :, 0])
    outgoing = jnp.where(upper_half, paired[:, :, 0], paired[:, :, 1])
    return (kept_half, outgoing)


def return_pairs(grad_pair, level_num, position):
    shaped = block_view(grad_pair, level_num)
    for bit_index in range(level_num):
        kept_half, outgoing = halve_blocks(shaped, bit_index, position)
        shaped = kept_half + from_partner(outgoing.astype(jnp.bfloat16), "seq", bit_index).astype(
            outgoing.dtype
        )
    return shaped[:, 0]


def body(query_states, key_states, value_states, out_grad, head_offsets):
    slab_rows = query_states.shape[0]
    head_count = head_offsets.shape[0]
    head_size = query_states.shape[1] // head_count
    softmax_scale = head_size ** (-0.5)
    queries = query_states.reshape(slab_rows, head_count, head_size)
    keys_own = key_states.reshape(slab_rows, head_count, head_size)
    values_own = value_states.reshape(slab_rows, head_count, head_size)
    grads = out_grad.reshape(slab_rows, head_count, head_size)
    position = lax.axis_index("seq")
    devices = lax.axis_size("seq")
    reach_slabs = WINDOW // slab_rows
    own_pair = jnp.stack([keys_own, values_own])
    earlier = []
    for shift_by in range(reach_slabs, 0, -1):
        earlier.append(passed_along(own_pair, "seq", shift_by))
    near_pair = jnp.concatenate(earlier + [own_pair], axis=1)
    span_cols = (reach_slabs + 1) * slab_rows
    local_rows = jnp.arange(slab_rows, dtype=jnp.int32)[:, None]
    key_cols = jnp.arange(span_cols, dtype=jnp.int32)[None, :]
    distance = local_rows - key_cols + reach_slabs * slab_rows
    near_allowed = (
        (distance >= 0)
        & (distance < WINDOW)
        & (position * slab_rows + key_cols - reach_slabs * slab_rows >= 0)
    )
    stats = forward_part(queries, near_pair[0], near_pair[1], near_allowed, softmax_scale)
    level_count = devices.bit_length() - 1
    saved = []
    for level_num in range(1, level_count + 1):
        stride = 2**level_num
        sparse_rows = slab_rows // stride
        chosen = jnp.arange(stride, dtype=jnp.int32)[:, None] == (head_offsets % stride)[None, :]
        sparse_pair = jnp.stack([pick_rows(keys_own, chosen), pick_rows(values_own, chosen)])
        group_pair = gather_pairs(sparse_pair, level_num, position)
        query_index = position % stride * sparse_rows + jnp.arange(sparse_rows, dtype=jnp.int32)
        level_allowed = jnp.arange(slab_rows, dtype=jnp.int32)[None, :] <= query_index[:, None]
        sparse_queries = pick_rows(queries, chosen)
        update = forward_part(
            sparse_queries, group_pair[0], group_pair[1], level_allowed, softmax_scale
        )
        current = tuple((pick_rows(member, chosen) for member in stats))
        merged = merge_stats(current, update)
        stats = tuple((put_rows(member, chosen, fresh) for member, fresh in zip(stats, merged)))
        saved.append((chosen, sparse_queries, group_pair, level_allowed, level_num))
    log_norm = stats[0] + jnp.log(stats[1])
    out_rows = stats[2] / stats[1][..., None]
    grad_dot = jnp.sum(grads.astype(jnp.float32) * out_rows, axis=-1)
    grad_query, near_key_grad, near_value_grad = backward_part(
        queries, near_pair[0], near_pair[1], grads, near_allowed, log_norm, grad_dot, softmax_scale
    )
    near_grads = jnp.stack([near_key_grad, near_value_grad])
    kv_grads = near_grads[:, reach_slabs * slab_rows :]
    for shift_by in range(1, reach_slabs + 1):
        block_start = (reach_slabs - shift_by) * slab_rows
        kv_grads = kv_grads + passed_along(
            near_grads[:, block_start : block_start + slab_rows], "seq", -shift_by
        )
    for chosen, sparse_queries, group_pair, level_allowed, level_num in saved:
        sparse_grads = pick_rows(grads, chosen)
        level_query, level_key, level_value = backward_part(
            sparse_queries,
            group_pair[0],
            group_pair[1],
            sparse_grads,
            level_allowed,
            pick_rows(log_norm, chosen),
            pick_rows(grad_dot, chosen),
            softmax_scale,
        )
        grad_query = add_rows(grad_query, chosen, level_query)
        returned = return_pairs(jnp.stack([level_key, level_value]), level_num, position)
        kv_grads = jnp.stack(
            [add_rows(kv_grads[0], chosen, returned[0]), add_rows(kv_grads[1], chosen, returned[1])]
        )
    shape_out = (slab_rows, head_count * head_size)
    return (
        grad_query.astype(jnp.bfloat16).reshape(shape_out),
        kv_grads[0].astype(jnp.bfloat16).reshape(shape_out),
        kv_grads[1].astype(jnp.bfloat16).reshape(shape_out),
    )


def solution(mesh):
    in_specs = (
        P(("batch", "seq"), "head"),
        P(("batch", "seq"), "head"),
        P(("batch", "seq"), "head"),
        P(("batch", "seq"), "head"),
        P("head"),
    )
    out_specs = (
        P(("batch", "seq"), "head"),
        P(("batch", "seq"), "head"),
        P(("batch", "seq"), "head"),
    )
    return jax.shard_map(body, mesh=mesh, in_specs=in_specs, out_specs=out_specs, check_vma=False)
```

profile of v0, /device:TPU:0, one launch (start us, length us, event | category | flops | bytes accessed | tf_op | source)
XLA Modules:
  0.0 341.8 jit_solution(2286592988269690056)
XLA Ops:
  4.1 6.7 %collective-permute-start = (bf16[2,256,4,128]{3,1,2,0:T(8,128)(2,1)}, bf16[2,256,4,128]{3,1,2,0:T(8,128)(2,1)}, u32[]{:S(2)}, u32[]{:S(2)}) collective-permute-start(bf16[2,256,4,128]{3,1,2,0:T(8,128)(2,1)} %pad_maximum_fusion.4), channel_id=1, source_target_pairs={{0,16},{4,20},{8,24},{12,28},{1,17},{5,21},{9,25},{13,29},{2,18},{... | collective-permute-start | bytes 1572872 | tf_op jit(solution)/shard_map/ppermute | solution.py:25
  10.9 5.2 %collective-permute-start.1 = (bf16[2,256,4,128]{3,1,2,0:T(8,128)(2,1)}, bf16[2,256,4,128]{3,1,2,0:T(8,128)(2,1)}, u32[]{:S(2)}, u32[]{:S(2)}) collective-permute-start(bf16[2,256,4,128]{3,1,2,0:T(8,128)(2,1)} %pad_maximum_fusion.4), channel_id=1, source_target_pairs={{0,12},{4,16},{8,20},{12,24},{16,28},{1,13},{5,17},{9,21},{13,25},... | collective-permute-start | bytes 1572872 | tf_op jit(solution)/shard_map/ppermute | solution.py:25
  16.2 1.6 fusion.72
  18.4 1.4 select_reduce_fusion.3
  19.8 2.1 collective-permute-start.5
  28.3 1.5 copy.1055
  29.8 1.5 copy.1054
  34.8 3.9 %collective-permute-start.2 = (bf16[2,256,4,128]{3,1,2,0:T(8,128)(2,1)}, bf16[2,256,4,128]{3,1,2,0:T(8,128)(2,1)S(1)}, u32[]{:S(2)}, u32[]{:S(2)}) collective-permute-start(bf16[2,256,4,128]{3,1,2,0:T(8,128)(2,1)} %pad_maximum_fusion.4), channel_id=1, source_target_pairs={{0,8},{4,12},{8,16},{12,20},{16,24},{20,28},{1,9},{5,13},{9,17},{1... | collective-permute-start | bytes 1572872 | tf_op jit(solution)/shard_map/ppermute | solution.py:25
  38.9 4.1 %collective-permute-start.3 = (bf16[2,256,4,128]{3,1,2,0:T(8,128)(2,1)}, bf16[2,256,4,128]{3,1,2,0:T(8,128)(2,1)S(1)}, u32[]{:S(2)}, u32[]{:S(2)}) collective-permute-start(bf16[2,256,4,128]{3,1,2,0:T(8,128)(2,1)} %pad_maximum_fusion.4), channel_id=1, source_target_pairs={{0,4},{4,8},{8,12},{12,16},{16,20},{20,24},{24,28},{1,5},{5,9},{9,... | collective-permute-start | bytes 1572872 | tf_op jit(solution)/shard_map/ppermute | solution.py:25
  45.6 8.7 %collective-permute-done.6 = bf16[2,128,4,128]{3,1,2,0:T(8,128)(2,1)S(1)} collective-permute-done((bf16[2,128,4,128]{3,1,2,0:T(8,128)(2,1)S(1)}, bf16[2,128,4,128]{3,1,2,0:T(8,128)(2,1)S(1)}, u32[]{:S(2)}, u32[]{:S(2)}) %collective-permute-start.6) | collective-permute-done | bytes 262176 | tf_op jit(solution)/shard_map/ppermute | solution.py:19
  54.3 1.8 collective-permute-start.9
  57.3 10.0 %collective-permute-done.9 = bf16[2,128,4,128]{3,1,2,0:T(8,128)(2,1)S(1)} collective-permute-done((bf16[2,128,4,128]{3,1,2,0:T(8,128)(2,1)S(1)}, bf16[2,128,4,128]{3,1,2,0:T(8,128)(2,1)S(1)}, u32[]{:S(2)}, u32[]{:S(2)}) %collective-permute-start.9) | collective-permute-done | bytes 262176 | tf_op jit(solution)/shard_map/ppermute | solution.py:19
  79.9 1.6 select_reduce_fusion.7
  95.4 1.9 select_reduce_fusion.2
  98.3 1.7 fusion.31
  101.2 1.8 select_reduce_fusion.1
  104.6 1.8 select_reduce_fusion
  110.9 2.1 copy.1071
  113.0 1.6 multiply_reduce_fusion
  120.7 1.9 copy.1077
  128.0 3.7 %convolution_bitcast_fusion = f32[1,1280,4,128]{1,3,2,0:T(8,128)S(1)} fusion(bf16[256,4,128]{0,2,1:T(8,128)(2,1)S(1)} %bitcast.393, f32[4,256,1280]{1,2,0:T(8,128)} %copy-done, f32[4,256]{1,0:T(4,128)S(1)} %bitcast.425), kind=kOutput, calls=%fused_computation.18 | convolution fusion | flops 338165760 | bytes 8130560 | tf_op jit(solution)/shard_map/hqk,qhd->khd/dot_general | solution.py:50
  131.8 2.6 fusion
  138.6 1.8 broadcast_in_dim.646
  140.3 2.1 copy.1085
  144.5 2.0 copy.1083
  146.6 4.4 %fusion.4 = f32[1,1280,4,128]{1,3,2,0:T(8,128)} fusion(bf16[4,256,1280]{1,2,0:T(8,128)(2,1)} %fusion, bf16[256,4,128]{0,2,1:T(8,128)(2,1)} %bitcast.414), kind=kOutput, calls=%fused_computation.17 | convolution fusion | flops 336199680 | bytes 5505024 | tf_op jit(solution)/shard_map/hqk,qhd->khd/dot_general | solution.py:60
  151.0 1.9 fusion.26
  154.9 2.0 copy.1099
  157.0 1.8 fusion.69
  158.8 31.9 %collective-permute-start.15 = (bf16[2,2,64,4,128]{4,2,1,3,0:T(8,128)(2,1)}, bf16[2,2,64,4,128]{4,2,1,3,0:T(8,128)(2,1)}, u32[]{:S(2)}, u32[]{:S(2)}) collective-permute-start(bf16[2,2,64,4,128]{4,2,1,3,0:T(8,128)(2,1)} %fusion.69), channel_id=1, source_target_pairs={{0,4},{4,0},{8,12},{12,8},{16,20},{20,16},{24,28},{28,24},{1,5},{5... | collective-permute-start | bytes 786440 | tf_op jit(solution)/shard_map/ppermute | solution.py:19
  190.6 3.7 %fusion.49 = (f32[2,256,4,128]{1,3,2,0:T(8,128)}, f32[2,256,4,128]{1,3,2,0:T(8,128)}, f32[2,256,4,128]{1,3,2,0:T(8,128)}, f32[2,256,4,128]{1,3,2,0:T(8,128)}) fusion(f32[1,1280,4,128]{1,3,2,0:T(8,128)} %fusion.4, f32[1,1280,4,128]{1,3,2,0:T(8,128)S(1)} %convolution_bitcast_fusion), kind=kLoop, calls=%fused_computation.81 | loop fusion | flops 1048576 | bytes 9437184 | tf_op jit(solution)/shard_map/stack | solution.py:185
  195.6 1.3 collective-permute-start.12
  196.9 1.6 collective-permute-start.11
  198.5 2.1 stack.80
  200.6 2.1 copy.1094
  202.7 2.1 stack.79
  204.8 2.0 copy.1093
  208.2 2.1 copy.1110
  211.3 2.1 copy.1108
  213.4 1.4 fusion.70
  214.8 12.6 %collective-permute-done.14 = bf16[2,1,128,4,128]{4,2,3,1,0:T(8,128)(2,1)} collective-permute-done((bf16[2,1,128,4,128]{4,2,3,1,0:T(8,128)(2,1)S(1)}, bf16[2,1,128,4,128]{4,2,3,1,0:T(8,128)(2,1)}, u32[]{:S(2)}, u32[]{:S(2)}) %collective-permute-start.14) | collective-permute-done | bytes 262176 | tf_op jit(solution)/shard_map/ppermute | solution.py:19
  227.4 1.3 bitcast_add_fusion.2
  228.8 6.8 %collective-permute-done.17 = bf16[2,4,32,4,128]{4,2,1,3,0:T(8,128)(2,1)S(1)} collective-permute-done((bf16[2,4,32,4,128]{4,2,1,3,0:T(8,128)(2,1)S(1)}, bf16[2,4,32,4,128]{4,2,1,3,0:T(8,128)(2,1)S(1)}, u32[]{:S(2)}, u32[]{:S(2)}) %collective-permute-start.17) | collective-permute-done | bytes 262176 | tf_op jit(solution)/shard_map/ppermute | solution.py:19
  238.2 11.8 %collective-permute-start.18 = (bf16[2,2,32,4,128]{4,2,3,1,0:T(8,128)(2,1)S(1)}, bf16[2,2,32,4,128]{4,2,3,1,0:T(8,128)(2,1)S(1)}, u32[]{:S(2)}, u32[]{:S(2)}) collective-permute-start(bf16[2,2,32,4,128]{4,2,3,1,0:T(8,128)(2,1)S(1)} %fusion.84), channel_id=1, source_target_pairs={{0,8},{8,0},{4,12},{12,4},{16,24},{24,16},{20,28},{28,20},{1,9},{9... | collective-permute-start | bytes 393224 | tf_op jit(solution)/shard_map/ppermute | solution.py:19
  251.1 59.0 %collective-permute-done.18 = bf16[2,2,32,4,128]{4,2,3,1,0:T(8,128)(2,1)S(1)} collective-permute-done((bf16[2,2,32,4,128]{4,2,3,1,0:T(8,128)(2,1)S(1)}, bf16[2,2,32,4,128]{4,2,3,1,0:T(8,128)(2,1)S(1)}, u32[]{:S(2)}, u32[]{:S(2)}) %collective-permute-start.18) | collective-permute-done | bytes 131104 | tf_op jit(solution)/shard_map/ppermute | solution.py:19
  310.2 4.9 %collective-permute-done.16 = bf16[2,1,64,4,128]{4,2,3,0,1:T(8,128)(2,1)S(1)} collective-permute-done((bf16[2,1,64,4,128]{4,2,3,0,1:T(8,128)(2,1)S(1)}, bf16[2,1,64,4,128]{4,2,3,0,1:T(8,128)(2,1)S(1)}, u32[]{:S(2)}, u32[]{:S(2)}) %collective-permute-start.16) | collective-permute-done | bytes 131104 | tf_op jit(solution)/shard_map/ppermute | solution.py:19
  315.3 21.5 %collective-permute-done.19 = bf16[2,1,32,4,128]{4,2,3,0,1:T(8,128)(2,1)S(1)} collective-permute-done((bf16[2,1,32,4,128]{4,2,3,0,1:T(8,128)(2,1)S(1)}, bf16[2,1,32,4,128]{4,2,3,0,1:T(8,128)(2,1)S(1)}, u32[]{:S(2)}, u32[]{:S(2)}) %collective-permute-start.19) | collective-permute-done | bytes 65568 | tf_op jit(solution)/shard_map/ppermute | solution.py:19
  337.0 2.3 fusion.48
  (336 shorter events, 81.8 us)
Async XLA Ops:
  0.6 15.6 %copy-start.10 = (bf16[256,512]{1,0:T(8,128)(2,1)S(1)}, bf16[256,512]{1,0:T(8,128)(2,1)}, u32[]{:S(2)}) copy-start(bf16[256,512]{1,0:T(8,128)(2,1)} %param.7) | copy-start | bytes 786436
  0.6 15.6 %copy-start.9 = (bf16[256,512]{1,0:T(8,128)(2,1)S(1)}, bf16[256,512]{1,0:T(8,128)(2,1)}, u32[]{:S(2)}) copy-start(bf16[256,512]{1,0:T(8,128)(2,1)} %param.6) | copy-start | bytes 786436
  0.7 15.5 %copy-start.61 = (s32[4]{0:T(128)S(1)}, s32[4]{0:T(128)}, u32[]{:S(2)}) copy-start(s32[4]{0:T(128)} %param.9) | copy-start | bytes 52
  0.7 15.5 %copy-start.11 = (bf16[256,512]{1,0:T(8,128)(2,1)S(1)}, bf16[256,512]{1,0:T(8,128)(2,1)}, u32[]{:S(2)}) copy-start(bf16[256,512]{1,0:T(8,128)(2,1)} %param.8) | copy-start | bytes 786436
  0.7 15.5 %copy-start.12 = (bf16[256,512]{1,0:T(8,128)(2,1)S(1)}, bf16[256,512]{1,0:T(8,128)(2,1)}, u32[]{:S(2)}) copy-start(bf16[256,512]{1,0:T(8,128)(2,1)} %param.5) | copy-start | bytes 786436
  4.1 64.4 %collective-permute-start = (bf16[2,256,4,128]{3,1,2,0:T(8,128)(2,1)}, bf16[2,256,4,128]{3,1,2,0:T(8,128)(2,1)}, u32[]{:S(2)}, u32[]{:S(2)}) collective-permute-start(bf16[2,256,4,128]{3,1,2,0:T(8,128)(2,1)} %pad_maximum_fusion.4), channel_id=1, source_target_pairs={{0,16},{4,20},{8,24},{12,28},{1,17},{5,21},{9,25},{13,29},{2,18},{... | collective-permute-start | bytes 1572872 | tf_op jit(solution)/shard_map/ppermute | solution.py:25
  10.9 58.8 %collective-permute-start.1 = (bf16[2,256,4,128]{3,1,2,0:T(8,128)(2,1)}, bf16[2,256,4,128]{3,1,2,0:T(8,128)(2,1)}, u32[]{:S(2)}, u32[]{:S(2)}) collective-permute-start(bf16[2,256,4,128]{3,1,2,0:T(8,128)(2,1)} %pad_maximum_fusion.4), channel_id=1, source_target_pairs={{0,12},{4,16},{8,20},{12,24},{16,28},{1,13},{5,17},{9,21},{13,25},... | collective-permute-start | bytes 1572872 | tf_op jit(solution)/shard_map/ppermute | solution.py:25
  16.2 9.7 %copy-start.58 = (pred[8,4]{0,1:T(4,128)(4,1)}, pred[8,4]{0,1:T(4,128)(4,1)S(1)}, u32[]{:S(2)}) copy-start(pred[8,4]{0,1:T(4,128)(4,1)S(1)} %iota_compare_fusion.5) | copy-start | bytes 100
  17.8 6.9 %collective-permute-start.7 = (bf16[2,32,4,128]{3,1,2,0:T(8,128)(2,1)S(1)}, bf16[2,32,4,128]{3,1,2,0:T(8,128)(2,1)S(1)}, u32[]{:S(2)}, u32[]{:S(2)}) collective-permute-start(bf16[2,32,4,128]{3,1,2,0:T(8,128)(2,1)S(1)} %pad_maximum_fusion.7), channel_id=1, source_target_pairs={{0,4},{4,0},{8,12},{12,8},{16,20},{20,16},{24,28},{28,24},{1,5},{5... | collective-permute-start | bytes 196616 | tf_op jit(solution)/shard_map/ppermute | solution.py:19
  18.2 8.6 %copy-start.60 = (pred[4,4]{0,1:T(4,128)(4,1)}, pred[4,4]{0,1:T(4,128)(4,1)S(1)}, u32[]{:S(2)}) copy-start(pred[4,4]{0,1:T(4,128)(4,1)S(1)} %iota_compare_fusion.4) | copy-start | bytes 52
  19.8 36.5 %copy-start.36 = (bf16[64,4,128]{2,1,0:T(4,128)(2,1)}, bf16[64,4,128]{2,1,0:T(4,128)(2,1)S(1)}, u32[]{:S(2)}) copy-start(bf16[64,4,128]{2,1,0:T(4,128)(2,1)S(1)} %get-tuple-element.49) | copy-start | bytes 196612
  19.8 15.0 %collective-permute-start.5 = (bf16[2,64,4,128]{3,1,2,0:T(8,128)(2,1)S(1)}, bf16[2,64,4,128]{3,1,2,0:T(8,128)(2,1)S(1)}, u32[]{:S(2)}, u32[]{:S(2)}) collective-permute-start(bf16[2,64,4,128]{3,1,2,0:T(8,128)(2,1)S(1)} %pad_maximum_fusion.6), channel_id=1, source_target_pairs={{0,4},{4,0},{8,12},{12,8},{16,20},{20,16},{24,28},{28,24},{1,5},{5... | collective-permute-start | bytes 393224 | tf_op jit(solution)/shard_map/ppermute | solution.py:19
  23.4 19.7 %collective-permute-start.4 = (bf16[2,128,4,128]{3,1,2,0:T(8,128)(2,1)S(1)}, bf16[2,128,4,128]{3,1,2,0:T(8,128)(2,1)S(1)}, u32[]{:S(2)}, u32[]{:S(2)}) collective-permute-start(bf16[2,128,4,128]{3,1,2,0:T(8,128)(2,1)S(1)} %pad_maximum_fusion.5), channel_id=1, source_target_pairs={{0,4},{4,0},{8,12},{12,8},{16,20},{20,16},{24,28},{28,24},{1,5},{5... | collective-permute-start | bytes 786440 | tf_op jit(solution)/shard_map/ppermute | solution.py:19
  24.8 14.1 %collective-permute-start.8 = (bf16[2,64,4,128]{3,1,2,0:T(8,128)(2,1)S(1)}, bf16[2,64,4,128]{3,1,2,0:T(8,128)(2,1)S(1)}, u32[]{:S(2)}, u32[]{:S(2)}) collective-permute-start(bf16[2,64,4,128]{3,1,2,0:T(8,128)(2,1)S(1)} %maximum_select_fusion.5), channel_id=1, source_target_pairs={{0,8},{8,0},{4,12},{12,4},{16,24},{24,16},{20,28},{28,20},{1,9},{9... | collective-permute-start | bytes 393224 | tf_op jit(solution)/shard_map/ppermute | solution.py:19
  26.9 7.9 %copy-start.43 = (pred[256,4]{0,1:T(4,128)(4,1)}, pred[256,4]{0,1:T(4,128)(4,1)S(1)}, u32[]{:S(2)}) copy-start(pred[256,4]{0,1:T(4,128)(4,1)S(1)} %broadcast_in_dim.591) | copy-start | bytes 3076
  27.0 17.8 %copy-start.24 = (pred[128,2,4]{1,0,2:T(8,128)(4,1)}, pred[128,2,4]{1,0,2:T(8,128)(4,1)S(1)}, u32[]{:S(2)}) copy-start(pred[128,2,4]{1,0,2:T(8,128)(4,1)S(1)} %broadcast_in_dim.594) | copy-start | bytes 3076
  27.2 7.6 %copy-start.45 = (pred[256,4]{0,1:T(4,128)(4,1)}, pred[256,4]{0,1:T(4,128)(4,1)S(1)}, u32[]{:S(2)}) copy-start(pred[256,4]{0,1:T(4,128)(4,1)S(1)} %broadcast_in_dim.616) | copy-start | bytes 3076
  28.3 17.3 %copy-start.17 = (bf16[128,4,128]{0,2,1:T(8,128)(2,1)}, bf16[128,4,128]{0,2,1:T(8,128)(2,1)S(1)}, u32[]{:S(2)}) copy-start(bf16[128,4,128]{0,2,1:T(8,128)(2,1)S(1)} %copy.1091) | copy-start | bytes 393220
  34.8 36.0 %collective-permute-start.2 = (bf16[2,256,4,128]{3,1,2,0:T(8,128)(2,1)}, bf16[2,256,4,128]{3,1,2,0:T(8,128)(2,1)S(1)}, u32[]{:S(2)}, u32[]{:S(2)}) collective-permute-start(bf16[2,256,4,128]{3,1,2,0:T(8,128)(2,1)} %pad_maximum_fusion.4), channel_id=1, source_target_pairs={{0,8},{4,12},{8,16},{12,20},{16,24},{20,28},{1,9},{5,13},{9,17},{1... | collective-permute-start | bytes 1572872 | tf_op jit(solution)/shard_map/ppermute | solution.py:25
  38.9 32.0 %collective-permute-start.3 = (bf16[2,256,4,128]{3,1,2,0:T(8,128)(2,1)}, bf16[2,256,4,128]{3,1,2,0:T(8,128)(2,1)S(1)}, u32[]{:S(2)}, u32[]{:S(2)}) collective-permute-start(bf16[2,256,4,128]{3,1,2,0:T(8,128)(2,1)} %pad_maximum_fusion.4), channel_id=1, source_target_pairs={{0,4},{4,8},{8,12},{12,16},{16,20},{20,24},{24,28},{1,5},{5,9},{9,... | collective-permute-start | bytes 1572872 | tf_op jit(solution)/shard_map/ppermute | solution.py:25
  43.1 24.4 %copy-start.39 = (bf16[32,4,128]{2,1,0:T(4,128)(2,1)S(1)}, bf16[32,4,128]{2,1,0:T(4,128)(2,1)}, u32[]{:S(2)}) copy-start(bf16[32,4,128]{2,1,0:T(4,128)(2,1)} %get-tuple-element.55) | copy-start | bytes 98308
  43.1 11.2 %collective-permute-start.6 = (bf16[2,128,4,128]{3,1,2,0:T(8,128)(2,1)S(1)}, bf16[2,128,4,128]{3,1,2,0:T(8,128)(2,1)S(1)}, u32[]{:S(2)}, u32[]{:S(2)}) collective-permute-start(bf16[2,128,4,128]{3,1,2,0:T(8,128)(2,1)S(1)} %maximum_select_fusion.3), channel_id=1, source_target_pairs={{0,8},{8,0},{4,12},{12,4},{16,24},{24,16},{20,28},{28,20},{1,9},{9... | collective-permute-start | bytes 786440 | tf_op jit(solution)/shard_map/ppermute | solution.py:19
  54.3 13.0 %collective-permute-start.9 = (bf16[2,128,4,128]{3,1,2,0:T(8,128)(2,1)S(1)}, bf16[2,128,4,128]{3,1,2,0:T(8,128)(2,1)S(1)}, u32[]{:S(2)}, u32[]{:S(2)}) collective-permute-start(bf16[2,128,4,128]{3,1,2,0:T(8,128)(2,1)S(1)} %maximum_select_fusion.4), channel_id=1, source_target_pairs={{0,16},{16,0},{4,20},{20,4},{8,24},{24,8},{12,28},{28,12},{1,17},{... | collective-permute-start | bytes 786440 | tf_op jit(solution)/shard_map/ppermute | solution.py:19
  56.2 14.7 %copy-start.13 = (bf16[2,256,4,128]{3,1,2,0:T(8,128)(2,1)}, bf16[2,256,4,128]{3,1,2,0:T(8,128)(2,1)S(1)}, u32[]{:S(2)}) copy-start(bf16[2,256,4,128]{3,1,2,0:T(8,128)(2,1)S(1)} %maximum_select_fusion.1) | copy-start | bytes 1572868
  56.6 14.4 %copy-start.49 = (f32[4,64]{1,0:T(4,128)}, f32[4,64]{1,0:T(4,128)S(1)}, u32[]{:S(2)}) copy-start(f32[4,64]{1,0:T(4,128)S(1)} %get-tuple-element.97) | copy-start | bytes 3076
  67.8 22.4 %copy-start.47 = (f32[4,32]{1,0:T(4,128)}, f32[4,32]{1,0:T(4,128)S(1)}, u32[]{:S(2)}) copy-start(f32[4,32]{1,0:T(4,128)S(1)} %get-tuple-element.99) | copy-start | bytes 1540
  78.3 10.2 %copy-start.31 = (f32[64,4,4]{1,0,2:T(8,128)S(1)}, f32[64,4,4]{1,0,2:T(8,128)}, u32[]{:S(2)}) copy-start(f32[64,4,4]{1,0,2:T(8,128)} %reshape.735) | copy-start | bytes 12292
  95.2 7.9 %copy-start.50 = (f32[4,64]{1,0:T(4,128)S(1)}, f32[4,64]{1,0:T(4,128)}, u32[]{:S(2)}) copy-start(f32[4,64]{1,0:T(4,128)} %copy-done.49) | copy-start | bytes 3076
  95.2 8.0 %copy-start.51 = (f32[64,4]{0,1:T(4,128)S(1)}, f32[64,4]{0,1:T(4,128)}, u32[]{:S(2)}) copy-start(f32[64,4]{0,1:T(4,128)} %get-tuple-element.66) | copy-start | bytes 3076
  110.9 7.7 %copy-start.14 = (bf16[2,256,4,128]{3,1,2,0:T(8,128)(2,1)S(1)}, bf16[2,256,4,128]{3,1,2,0:T(8,128)(2,1)}, u32[]{:S(2)}) copy-start(bf16[2,256,4,128]{3,1,2,0:T(8,128)(2,1)} %copy-done.13) | copy-start | bytes 1572868
  114.5 10.0 %copy-start.15 = (bf16[128,4,128]{0,2,1:T(8,128)(2,1)S(1)}, bf16[128,4,128]{0,2,1:T(8,128)(2,1)}, u32[]{:S(2)}) copy-start(bf16[128,4,128]{0,2,1:T(8,128)(2,1)} %copy.1092) | copy-start | bytes 393220
  158.8 79.5 %collective-permute-start.15 = (bf16[2,2,64,4,128]{4,2,1,3,0:T(8,128)(2,1)}, bf16[2,2,64,4,128]{4,2,1,3,0:T(8,128)(2,1)}, u32[]{:S(2)}, u32[]{:S(2)}) collective-permute-start(bf16[2,2,64,4,128]{4,2,1,3,0:T(8,128)(2,1)} %fusion.69), channel_id=1, source_target_pairs={{0,4},{4,0},{8,12},{12,8},{16,20},{20,16},{24,28},{28,24},{1,5},{5... | collective-permute-start | bytes 786440 | tf_op jit(solution)/shard_map/ppermute | solution.py:19
  194.3 142.6 %collective-permute-start.13 = (f32[2,256,4,128]{1,3,2,0:T(8,128)}, f32[2,256,4,128]{1,3,2,0:T(8,128)}, u32[]{:S(2)}, u32[]{:S(2)}) collective-permute-start(f32[2,256,4,128]{1,3,2,0:T(8,128)} %get-tuple-element.73), channel_id=1, source_target_pairs={{16,0},{20,4},{24,8},{28,12},{17,1},{21,5},{25,9},{29,13},{18,2},{... | collective-permute-start | bytes 3145736 | tf_op jit(solution)/shard_map/ppermute | solution.py:25
  195.6 141.4 %collective-permute-start.12 = (f32[2,256,4,128]{1,3,2,0:T(8,128)}, f32[2,256,4,128]{1,3,2,0:T(8,128)}, u32[]{:S(2)}, u32[]{:S(2)}) collective-permute-start(f32[2,256,4,128]{1,3,2,0:T(8,128)} %get-tuple-element.74), channel_id=1, source_target_pairs={{12,0},{16,4},{20,8},{24,12},{28,16},{13,1},{17,5},{21,9},{25,13},... | collective-permute-start | bytes 3145736 | tf_op jit(solution)/shard_map/ppermute | solution.py:25
  196.9 140.1 %collective-permute-start.11 = (f32[2,256,4,128]{1,3,2,0:T(8,128)}, f32[2,256,4,128]{1,3,2,0:T(8,128)}, u32[]{:S(2)}, u32[]{:S(2)}) collective-permute-start(f32[2,256,4,128]{1,3,2,0:T(8,128)} %get-tuple-element.72), channel_id=1, source_target_pairs={{8,0},{12,4},{16,8},{20,12},{24,16},{28,20},{9,1},{13,5},{17,9},{2... | collective-permute-start | bytes 3145736 | tf_op jit(solution)/shard_map/ppermute | solution.py:25
  200.6 9.6 %copy-start.23 = (bf16[4,32,256]{2,1,0:T(8,128)(2,1)S(1)}, bf16[4,32,256]{2,1,0:T(8,128)(2,1)}, u32[]{:S(2)}) copy-start(bf16[4,32,256]{2,1,0:T(8,128)(2,1)} %copy-done.22) | copy-start | bytes 196612
  200.6 9.6 %copy-start.40 = (bf16[32,4,128]{2,1,0:T(4,128)(2,1)S(1)}, bf16[32,4,128]{2,1,0:T(4,128)(2,1)}, u32[]{:S(2)}) copy-start(bf16[32,4,128]{2,1,0:T(4,128)(2,1)} %get-tuple-element.55) | copy-start | bytes 98308
  208.1 19.3 %collective-permute-start.14 = (bf16[2,1,128,4,128]{4,2,3,1,0:T(8,128)(2,1)S(1)}, bf16[2,1,128,4,128]{4,2,3,1,0:T(8,128)(2,1)}, u32[]{:S(2)}, u32[]{:S(2)}) collective-permute-start(bf16[2,1,128,4,128]{4,2,3,1,0:T(8,128)(2,1)S(1)} %fusion.68), channel_id=1, source_target_pairs={{0,4},{4,0},{8,12},{12,8},{16,20},{20,16},{24,28},{28,24},{1,5},{5... | collective-permute-start | bytes 786440 | tf_op jit(solution)/shard_map/ppermute | solution.py:19
  213.4 22.3 %copy-start.19 = (f32[2,256,4,128]{1,3,2,0:T(8,128)S(1)}, f32[2,256,4,128]{1,3,2,0:T(8,128)}, u32[]{:S(2)}) copy-start(f32[2,256,4,128]{1,3,2,0:T(8,128)} %get-tuple-element.71) | copy-start | bytes 3145732
  213.4 23.6 %copy-start.7 = (f32[256,4,128]{2,0,1:T(8,128)S(1)}, f32[256,4,128]{2,0,1:T(8,128)}, u32[]{:S(2)}) copy-start(f32[256,4,128]{2,0,1:T(8,128)} %copy.1110) | copy-start | bytes 1572868
  213.4 23.6 %copy-start.8 = (f32[256,4,128]{2,0,1:T(8,128)S(1)}, f32[256,4,128]{2,0,1:T(8,128)}, u32[]{:S(2)}) copy-start(f32[256,4,128]{2,0,1:T(8,128)} %copy.1108) | copy-start | bytes 1572868
  227.4 8.2 %collective-permute-start.17 = (bf16[2,4,32,4,128]{4,2,1,3,0:T(8,128)(2,1)S(1)}, bf16[2,4,32,4,128]{4,2,1,3,0:T(8,128)(2,1)S(1)}, u32[]{:S(2)}, u32[]{:S(2)}) collective-permute-start(bf16[2,4,32,4,128]{4,2,1,3,0:T(8,128)(2,1)S(1)} %fusion.70), channel_id=1, source_target_pairs={{0,4},{4,0},{8,12},{12,8},{16,20},{20,16},{24,28},{28,24},{1,5},{5... | collective-permute-start | bytes 786440 | tf_op jit(solution)/shard_map/ppermute | solution.py:19
  228.8 21.2 %copy-start.6 = (f32[256,4,128]{2,0,1:T(8,128)S(1)}, f32[256,4,128]{2,0,1:T(8,128)}, u32[]{:S(2)}) copy-start(f32[256,4,128]{2,0,1:T(8,128)} %copy.1099) | copy-start | bytes 1572868
  235.7 101.4 %collective-permute-start.10 = (f32[2,256,4,128]{1,3,2,0:T(8,128)S(1)}, f32[2,256,4,128]{1,3,2,0:T(8,128)S(1)}, u32[]{:S(2)}, u32[]{:S(2)}) collective-permute-start(f32[2,256,4,128]{1,3,2,0:T(8,128)S(1)} %copy-done.19), channel_id=1, source_target_pairs={{4,0},{8,4},{12,8},{16,12},{20,16},{24,20},{28,24},{5,1},{9,5},{13... | collective-permute-start | bytes 3145736 | tf_op jit(solution)/shard_map/ppermute | solution.py:25
  238.2 71.9 %collective-permute-start.18 = (bf16[2,2,32,4,128]{4,2,3,1,0:T(8,128)(2,1)S(1)}, bf16[2,2,32,4,128]{4,2,3,1,0:T(8,128)(2,1)S(1)}, u32[]{:S(2)}, u32[]{:S(2)}) collective-permute-start(bf16[2,2,32,4,128]{4,2,3,1,0:T(8,128)(2,1)S(1)} %fusion.84), channel_id=1, source_target_pairs={{0,8},{8,0},{4,12},{12,4},{16,24},{24,16},{20,28},{28,20},{1,9},{9... | collective-permute-start | bytes 393224 | tf_op jit(solution)/shard_map/ppermute | solution.py:19
  251.1 86.0 %copy-start.1 = (f32[1,1280,4,128]{1,3,2,0:T(8,128)S(1)}, f32[1,1280,4,128]{1,3,2,0:T(8,128)}, u32[]{:S(2)}) copy-start(f32[1,1280,4,128]{1,3,2,0:T(8,128)} %fusion.4) | copy-start | bytes 7864324
  310.1 5.0 %collective-permute-start.16 = (bf16[2,1,64,4,128]{4,2,3,0,1:T(8,128)(2,1)S(1)}, bf16[2,1,64,4,128]{4,2,3,0,1:T(8,128)(2,1)S(1)}, u32[]{:S(2)}, u32[]{:S(2)}) collective-permute-start(bf16[2,1,64,4,128]{4,2,3,0,1:T(8,128)(2,1)S(1)} %fusion.83), channel_id=1, source_target_pairs={{0,8},{8,0},{4,12},{12,4},{16,24},{24,16},{20,28},{28,20},{1,9},{9... | collective-permute-start | bytes 393224 | tf_op jit(solution)/shard_map/ppermute | solution.py:19
  315.1 21.7 %collective-permute-start.19 = (bf16[2,1,32,4,128]{4,2,3,0,1:T(8,128)(2,1)S(1)}, bf16[2,1,32,4,128]{4,2,3,0,1:T(8,128)(2,1)S(1)}, u32[]{:S(2)}, u32[]{:S(2)}) collective-permute-start(bf16[2,1,32,4,128]{4,2,3,0,1:T(8,128)(2,1)S(1)} %fusion.92), channel_id=1, source_target_pairs={{0,16},{16,0},{4,20},{20,4},{8,24},{24,8},{12,28},{28,12},{1,17},{... | collective-permute-start | bytes 196616 | tf_op jit(solution)/shard_map/ppermute | solution.py:19
  (36 other events, 137.1 us)
where the time goes:
time: 343 us; the launch traced here: 342 us
  waiting for transfers between devices  124 us (36%)
  starting transfers between devices  74.4 us (22%)
  local copies, waits for them, and re-layouts  72.4 us (21%)
  other arithmetic  41.4 us (12%)
  matrix products  27.8 us (8%)
    ppermute x12, waiting for transfers between devices, from_partner(): return lax.ppermute(block, axis, route)  124 us
    ppermute x12, starting transfers between devices, from_partner(): return lax.ppermute(block, axis, route)  49 us
    ppermute x8, starting transfers between devices, passed_along(): lax.ppermute(value, axis, [(source, source + steps) for source in range(l...  25.4 us
    reduce_sum x18, other arithmetic, pick_rows(): jnp.sum(jnp.where(row_mask(source, chosen), shaped, jnp.zeros((), source....  14.9 us
    broadcast_in_dim x32, local copies, waits for them, and re-layouts, put_rows(): jnp.where(row_mask(source, chosen), update[:, None], shaped)  12.7 us
    broadcast_in_dim x19, local copies, waits for them, and re-layouts, add_rows(): jnp.where(row_mask(source, chosen), update[:, None], 0.0)  10.7 us
    unnamed x138, local copies, waits for them, and re-layouts  9.49 us
    another operation x4, local copies, waits for them, and re-layouts, body(): jnp.stack([level_key, level_value])  8.35 us
  transfers between devices with their start and end apart: 20, of which 7 were waited for; matrix products, arithmetic and copies ran while one was open for 14% of the time, Pallas kernels for 0%

commit v1 on v0

v1 whole, which is shorter than its diff:
```python
import functools

import jax
import jax.numpy as jnp
from jax import lax
from jax.experimental import pallas as pl
from jax.experimental.pallas import tpu as pltpu
from jax.sharding import PartitionSpec as P

WINDOW = 1024
MASKED = -1e30


def contract(left, right, left_dim, right_dim):
    return lax.dot_general(
        left, right, (((left_dim,), (right_dim,)), ((), ())), preferred_element_type=jnp.float32
    )


def kernel(
    devices,
    batches,
    heads,
    off_ref,
    key_ref,
    value_ref,
    query_ref,
    grad_ref,
    dq_ref,
    dk_ref,
    dv_ref,
    kv,
    qg,
    scores,
    probs,
    level,
    total,
    dq_out,
    part_out,
    part_in,
    kv_out,
    in_send,
    kv_recv,
    qg_recv,
    peer_send,
    part_send,
    part_recv,
    out_send,
    out_recv,
):
    rows, width = query_ref.shape[0], query_ref.shape[1] // heads
    spots = devices // (heads * batches)
    group = spots * batches
    slots = devices // group
    level_count = devices.bit_length() - 1
    scale = width ** (-0.5)

    seq, batch = lax.axis_index("seq"), lax.axis_index("batch")
    unit = seq // spots
    head, sequence = unit // batches, unit % batches
    share = (seq % spots) * batches + batch
    home_share, home_slot = seq % group, seq // group
    at_home = (sequence == batch) & (home_share == share)

    def worker(h):
        place = {"seq": (h * batches + batch) * spots + home_share // batches}
        place["batch"] = home_share % batches
        return place, at_home & (head == h)

    def owner(t):
        return {"seq": share + group * t, "batch": sequence}, at_home & (home_slot == t)

    def peer(r):
        other = (share + r) % group
        return other, {"seq": unit * spots + other // batches, "batch": other % batches}

    def remote(src, dst, send_sem, recv_sem, place):
        return pltpu.make_async_remote_copy(
            src_ref=src,
            dst_ref=dst,
            send_sem=send_sem,
            recv_sem=recv_sem,
            device_id=place,
            device_id_type=pl.DeviceIdType.MESH,
        )

    def move(src, dst, send_sem, recv_sem, place, same):
        @pl.when(same)
        def _():
            pltpu.make_async_copy(src, dst, recv_sem).start()

        @pl.when(jnp.logical_not(same))
        def _():
            remote(src, dst, send_sem, recv_sem, place).start()

    def sent(src, dst, send_sem, recv_sem, place, same):
        @pl.when(jnp.logical_not(same))
        def _():
            remote(src, dst, send_sem, recv_sem, place).wait_send()

    def landed(ref, sem):
        pltpu.make_async_copy(ref, ref, sem).wait()

    barrier = pltpu.get_barrier_semaphore()

    def greet(place):
        pl.semaphore_signal(barrier, inc=1, device_id=place, device_id_type=pl.DeviceIdType.MESH)

    for place, same in [worker(h) for h in range(heads)] + [owner(t) for t in range(slots)]:
        pl.when(jnp.logical_not(same))(functools.partial(greet, place))
    for r in range(1, group):
        greet(peer(r)[1])
    own = jnp.where(at_home, 1, 0)
    pl.semaphore_wait(barrier, heads + slots - 2 * own + group - 1)

    def inward(a, h):
        source = (key_ref, value_ref, query_ref, grad_ref)[a]
        src = source.at[:, pl.ds(h * width, width)]
        if a < 2:
            dst, recv = kv.at[a, seq], kv_recv.at[a, seq]
        else:
            dst, recv = qg.at[a - 2, home_slot], qg_recv.at[a - 2, home_slot]
        return (src, dst, in_send.at[a, h], recv) + worker(h)

    for a in range(4):
        for h in range(heads):
            move(*inward(a, h))

    offset = off_ref[head]
    key_row = lax.broadcasted_iota(jnp.int32, (rows, rows), 0)
    query_row = lax.broadcasted_iota(jnp.int32, (rows, rows), 1)
    apart = (key_row ^ offset) | (query_row ^ offset)
    matched = jnp.zeros((rows, rows), jnp.float32)
    for l in range(1, level_count + 1):
        matched += jnp.where(apart & (2**l - 1) == 0, 1.0, 0.0)
    level[...] = matched

    def clear(j, _):
        total[0, j] = jnp.zeros((rows, width), jnp.float32)
        total[1, j] = jnp.zeros((rows, width), jnp.float32)
        return 0

    lax.fori_loop(0, devices, clear, 0)

    def shared(a, t, r):
        slab = share + group * t
        block = kv.at[a, slab]
        return remote(block, block, peer_send.at[r - 1, a, t], kv_recv.at[a, slab], peer(r)[1])

    for t in range(slots):
        for a in range(2):
            slab = share + group * t
            landed(kv.at[a, slab], kv_recv.at[a, slab])
            for r in range(1, group):
                shared(a, t, r).start()

    def outward(a, t):
        src = dq_out.at[t] if a == 0 else kv_out.at[a - 1, t]
        dst = (dq_ref, dk_ref, dv_ref)[a].at[:, pl.ds(pl.multiple_of(head * width, width), width)]
        return (src, dst, out_send.at[a, t], out_recv.at[a, head]) + owner(t)

    def work(t):
        slab = share + group * t
        for a in range(2):
            for r in range(1, group):
                other = peer(r)[0] + group * t
                landed(kv.at[a, other], kv_recv.at[a, other])
            landed(qg.at[a, t], qg_recv.at[a, t])
        query, grad = qg[0, t], qg[1, t]

        def score(j, row_max):
            s = contract(kv[0, j], query, 1, 1) * scale
            probs[j] = contract(kv[1, j], grad, 1, 1)
            ahead = (slab - j) * rows
            higher = jnp.int32(0)
            for l in range(1, level_count):
                higher += jnp.where((slab >> l) != (j >> l), 1, 0)
            distance = (
                lax.broadcasted_iota(jnp.int32, (rows, rows), 1)
                - lax.broadcasted_iota(jnp.int32, (rows, rows), 0)
                + ahead
            )
            near = jnp.where(distance < WINDOW, 1.0, 0.0)
            count = near + jnp.maximum(level[...] - higher.astype(jnp.float32), 0.0)
            count = jnp.where(distance >= 0, count, 0.0)
            s = jnp.where(count > 0.0, s + jnp.log(count), MASKED)
            scores[j] = s
            return jnp.maximum(row_max, jnp.max(s, axis=0, keepdims=True))

        blocks = group * (t + 1)
        row_max = lax.fori_loop(0, blocks, score, jnp.full((1, rows), MASKED, jnp.float32))

        def soften(j, carry):
            row_sum, row_dot = carry
            e = jnp.exp(scores[j] - row_max)
            scores[j] = e
            row_sum += jnp.sum(e, axis=0, keepdims=True)
            row_dot += jnp.sum(e * probs[j], axis=0, keepdims=True)
            return row_sum, row_dot

        zero = jnp.zeros((1, rows), jnp.float32)
        row_sum, row_dot = lax.fori_loop(0, blocks, soften, (zero, zero))
        inverse = 1.0 / row_sum
        grad_dot = row_dot * inverse

        def differentiate(j, dq):
            p = scores[j] * inverse
            ds = (p * (probs[j] - grad_dot)).astype(jnp.bfloat16)
            total[1, j] += contract(p.astype(jnp.bfloat16), grad, 1, 0)
            total[0, j] += contract(ds, query, 1, 0)
            return dq + contract(kv[0, j], ds, 0, 0)

        dq = lax.fori_loop(0, blocks, differentiate, jnp.zeros((width, rows), jnp.float32))
        dq_out[t] = (dq * scale).T.astype(jnp.bfloat16)
        move(*outward(0, t))

    for t in range(slots):
        work(t)

    factors = (scale, 1.0)

    def partial_sum(a, t, r):
        other, place = peer(r)
        return remote(
            part_out.at[r - 1, a, t],
            part_in.at[r - 1, a, t],
            part_send.at[r - 1, a, t],
            part_recv.at[r - 1, a, t],
            place,
        )

    for r in range(1, group):
        for t in range(slots):
            for a in range(2):
                value = total[a, peer(r)[0] + group * t] * factors[a]
                part_out[r - 1, a, t] = value.astype(jnp.bfloat16)
                partial_sum(a, t, r).start()
    for t in range(slots):
        for a in range(2):
            value = total[a, share + group * t] * factors[a]
            for r in range(1, group):
                partial_sum(a, t, r).wait_recv()
                value += part_in[r - 1, a, t].astype(jnp.float32)
            kv_out[a, t] = value.astype(jnp.bfloat16)
            move(*outward(a + 1, t))

    for a, ref in enumerate((dq_ref, dk_ref, dv_ref)):
        for h in range(heads):
            landed(ref.at[:, pl.ds(h * width, width)], out_recv.at[a, h])
        for t in range(slots):
            sent(*outward(a, t))
    for a in range(4):
        for h in range(heads):
            sent(*inward(a, h))
    for a in range(2):
        for t in range(slots):
            for r in range(1, group):
                shared(a, t, r).wait_send()
                partial_sum(a, t, r).wait_send()


def body(devices, batches, query_states, key_states, value_states, out_grad, head_offsets):
    rows, heads = query_states.shape[0], head_offsets.shape[0]
    width = query_states.shape[1] // heads
    group = devices // heads
    slots = devices // group
    half, full = jnp.bfloat16, jnp.float32
    anywhere = pl.BlockSpec(memory_space=pl.ANY)
    dma = pltpu.SemaphoreType.DMA
    result = jax.ShapeDtypeStruct(query_states.shape, half)
    return pl.pallas_call(
        functools.partial(kernel, devices, batches, heads),
        out_shape=(result,) * 3,
        in_specs=[pl.BlockSpec(memory_space=pltpu.SMEM)] + [anywhere] * 4,
        out_specs=(anywhere,) * 3,
        scratch_shapes=[
            pltpu.VMEM((2, devices, rows, width), half),
            pltpu.VMEM((2, slots, rows, width), half),
            pltpu.VMEM((devices, rows, rows), full),
            pltpu.VMEM((devices, rows, rows), full),
            pltpu.VMEM((rows, rows), full),
            pltpu.VMEM((2, devices, rows, width), full),
            pltpu.VMEM((slots, rows, width), half),
            pltpu.VMEM((group - 1, 2, slots, rows, width), half),
            pltpu.VMEM((group - 1, 2, slots, rows, width), half),
            pltpu.VMEM((2, slots, rows, width), half),
            dma((4, heads)),
            dma((2, devices)),
            dma((2, slots)),
            dma((group - 1, 2, slots)),
            dma((group - 1, 2, slots)),
            dma((group - 1, 2, slots)),
            dma((3, slots)),
            dma((3, heads)),
        ],
        compiler_params=pltpu.CompilerParams(
            collective_id=0, has_side_effects=True, vmem_limit_bytes=56 * 2**20
        ),
    )(head_offsets, key_states, value_states, query_states, out_grad)


def solution(mesh):
    slab = P(("batch", "seq"), "head")
    return jax.shard_map(
        functools.partial(body, mesh.shape["seq"], mesh.shape["batch"]),
        mesh=mesh,
        in_specs=(slab,) * 4 + (P("head"),),
        out_specs=(slab,) * 3,
        check_vma=False,
    )
```

time: 343 us -> 57.5 us (0.17)
  waiting for transfers between devices: 124 us -> 0 us
  starting transfers between devices: 74.4 us -> 0 us
  local copies, waits for them, and re-layouts: 72.4 us -> 3.46 us
  Pallas kernels: 0 us -> 52.6 us
  other arithmetic: 41.4 us -> 0 us
  matrix products: 27.8 us -> 0 us
    ppermute x20 -> x0, waiting for transfers between devices: 124 us -> none  [the longest x12 124 us: from_partner(): return lax.ppermute(block, axis, route)]
    ppermute x20 -> x0, starting transfers between devices: 74.4 us -> none  [the longest x12 49 us: from_partner(): return lax.ppermute(block, axis, route)]
    pallas_call x0 -> x1, Pallas kernels: none -> 52.6 us  [body(): pl.pallas_call(functools.partial(kernel, devices, batches, heads), out_sh...]
    dot_general x24 -> x0, matrix products: 27.8 us -> none  [the longest x4 7.58 us: backward_part(): jnp.einsum('hqk,qhd->khd', grad_scores, queries, preferred_element_type=j...]
    broadcast_in_dim x59 -> x0, local copies, waits for them, and re-layouts: 27.8 us -> none  [the longest x32 12.7 us: put_rows(): jnp.where(row_mask(source, chosen), update[:, None], shaped)]
    reduce_sum x23 -> x0, other arithmetic: 19.5 us -> none  [the longest x18 14.9 us: pick_rows(): jnp.sum(jnp.where(row_mask(source, chosen), shaped, jnp.zeros((), source....]
    another operation x19 -> x0, local copies, waits for them, and re-layouts: 9.67 us -> none  [the longest x4 8.35 us: body(): jnp.stack([level_key, level_value])]
    reshape x11 -> x0, local copies, waits for them, and re-layouts: 9.11 us -> none  [the longest x10 8.27 us: pick_rows(): source.reshape((source.shape[0] // stride, stride) + source.shape[1:])]
  transfers between devices with their start and end apart: 20 -> 0, of which waited for: 7 -> 0; matrix products, arithmetic and copies ran while one was open for 14% -> 0% of each run, Pallas kernels for 0% -> 0%
where the time goes in v1:
time: 57.5 us; the launch traced here: 56.8 us
  Pallas kernels  52.6 us (91%)
  local copies, waits for them, and re-layouts  3.46 us (6%)
  between operations  0.65 us (1%)
    pallas_call x1, Pallas kernels, body(): pl.pallas_call(functools.partial(kernel, devices, batches, heads), out_sh...  52.6 us
    unnamed x7, local copies, waits for them, and re-layouts  3.46 us

profile of v1, /device:TPU:0, one launch (start us, length us, event | category | flops | bytes accessed | tf_op | source)
XLA Modules:
  0.0 56.8 jit_solution(3990288185204051657)
XLA Ops:
  0.6 52.6 %shard_map.76 = (bf16[256,512]{1,0:T(8,128)(2,1)}, bf16[256,512]{1,0:T(8,128)(2,1)}, bf16[256,512]{1,0:T(8,128)(2,1)}) custom-call(s32[4]{0:T(128)} %off_ref.1, bf16[256,512]{1,0:T(8,128)(2,1)} %key_ref.1, bf16[256,512]{1,0:T(8,128)(2,1)} %value_ref.1, bf16[256,512]{1,0:T(8,128)(2,1)} %query_ref.1, bf16[256,512]{1,0:T(8,128)(2,1)} %grad_ref.1), custom_call_target="tpu_custom_call" | custom-call | tf_op jit(solution)/shard_map/pallas_call | solution.py:271
  53.3 0.0 copy-start.1
  53.3 1.7 %copy.11 = bf16[256,512]{1,0:T(8,128)(2,1)} copy(bf16[256,512]{1,0:T(8,128)(2,1)} %get-tuple-element.6) | data formatting | bytes 524288
  55.0 0.0 copy-done.1
  55.0 0.0 copy-start
  55.0 0.7 %copy.12 = bf16[256,512]{1,0:T(8,128)(2,1)} copy(bf16[256,512]{1,0:T(8,128)(2,1)S(1)} %copy-done.1) | data formatting | bytes 524288
  55.7 0.3 copy-done
  56.1 0.7 %copy.13 = bf16[256,512]{1,0:T(8,128)(2,1)} copy(bf16[256,512]{1,0:T(8,128)(2,1)S(1)} %copy-done) | data formatting | bytes 524288
Async XLA Ops:
  53.3 1.7 %copy-start.1 = (bf16[256,512]{1,0:T(8,128)(2,1)S(1)}, bf16[256,512]{1,0:T(8,128)(2,1)}, u32[]{:S(2)}) copy-start(bf16[256,512]{1,0:T(8,128)(2,1)} %get-tuple-element.7) | copy-start | bytes 786436
  55.0 1.0 %copy-start = (bf16[256,512]{1,0:T(8,128)(2,1)S(1)}, bf16[256,512]{1,0:T(8,128)(2,1)}, u32[]{:S(2)}) copy-start(bf16[256,512]{1,0:T(8,128)(2,1)} %get-tuple-element.8) | copy-start | bytes 786436

commit v2 on v1

--- a/solution.py
+++ b/solution.py
@@ -33,6 +33,7 @@
     qg,
     scores,
     probs,
+    tops,
     level,
     total,
     dq_out,
@@ -115,16 +116,21 @@
 
     def inward(a, h):
         source = (key_ref, value_ref, query_ref, grad_ref)[a]
-        src = source.at[:, pl.ds(h * width, width)]
+        src = source.at[:, pl.ds(pl.multiple_of(h * width, width), width)]
         if a < 2:
             dst, recv = kv.at[a, seq], kv_recv.at[a, seq]
         else:
             dst, recv = qg.at[a - 2, home_slot], qg_recv.at[a - 2, home_slot]
         return (src, dst, in_send.at[a, h], recv) + worker(h)
 
-    for a in range(4):
-        for h in range(heads):
-            move(*inward(a, h))
+    upward = head * 2 < heads
+
+    def far_first(step, count):
+        return jnp.where(upward, count - 1 - step, step)
+
+    for step in range(heads):
+        for a in range(4):
+            move(*inward(a, far_first(step, heads)))
 
     offset = off_ref[head]
     key_row = lax.broadcasted_iota(jnp.int32, (rows, rows), 0)
@@ -147,7 +153,7 @@
         block = kv.at[a, slab]
         return remote(block, block, peer_send.at[r - 1, a, t], kv_recv.at[a, slab], peer(r)[1])
 
-    for t in range(slots):
+    def share_out(t):
         for a in range(2):
             slab = share + group * t
             landed(kv.at[a, slab], kv_recv.at[a, slab])
@@ -168,9 +174,10 @@
             landed(qg.at[a, t], qg_recv.at[a, t])
         query, grad = qg[0, t], qg[1, t]
 
-        def score(j, row_max):
+        def score(j, carry):
+            row_max, row_sum, row_dot = carry
             s = contract(kv[0, j], query, 1, 1) * scale
-            probs[j] = contract(kv[1, j], grad, 1, 1)
+            grad_probs = contract(kv[1, j], grad, 1, 1)
             ahead = (slab - j) * rows
             higher = jnp.int32(0)
             for l in range(1, level_count):
@@ -183,59 +190,66 @@
             near = jnp.where(distance < WINDOW, 1.0, 0.0)
             count = near + jnp.maximum(level[...] - higher.astype(jnp.float32), 0.0)
             count = jnp.where(distance >= 0, count, 0.0)
-            s = jnp.where(count > 0.0, s + jnp.log(count), MASKED)
-            scores[j] = s
-            return jnp.maximum(row_max, jnp.max(s, axis=0, keepdims=True))
+            s = jnp.where(count > 0.0, s, MASKED)
+            top = jnp.maximum(row_max, jnp.max(s, axis=0, keepdims=True))
+            fade = jnp.exp(row_max - top)
+            e = count * jnp.exp(s - top)
+            scores[j] = e
+            probs[j] = grad_probs
+            tops[j] = top
+            row_sum = row_sum * fade + jnp.sum(e, axis=0, keepdims=True)
+            row_dot = row_dot * fade + jnp.sum(e * grad_probs, axis=0, keepdims=True)
+            return top, row_sum, row_dot
 
         blocks = group * (t + 1)
-        row_max = lax.fori_loop(0, blocks, score, jnp.full((1, rows), MASKED, jnp.float32))
-
-        def soften(j, carry):
-            row_sum, row_dot = carry
-            e = jnp.exp(scores[j] - row_max)
-            scores[j] = e
-            row_sum += jnp.sum(e, axis=0, keepdims=True)
-            row_dot += jnp.sum(e * probs[j], axis=0, keepdims=True)
-            return row_sum, row_dot
-
         zero = jnp.zeros((1, rows), jnp.float32)
-        row_sum, row_dot = lax.fori_loop(0, blocks, soften, (zero, zero))
+        start = (jnp.full((1, rows), MASKED, jnp.float32), zero, zero)
+        row_max, row_sum, row_dot = lax.fori_loop(0, blocks, score, start, unroll=2)
         inverse = 1.0 / row_sum
         grad_dot = row_dot * inverse
 
         def differentiate(j, dq):
-            p = scores[j] * inverse
+            p = scores[j] * (jnp.exp(tops[j] - row_max) * inverse)
             ds = (p * (probs[j] - grad_dot)).astype(jnp.bfloat16)
             total[1, j] += contract(p.astype(jnp.bfloat16), grad, 1, 0)
             total[0, j] += contract(ds, query, 1, 0)
             return dq + contract(kv[0, j], ds, 0, 0)
 
-        dq = lax.fori_loop(0, blocks, differentiate, jnp.zeros((width, rows), jnp.float32))
+        dq = jnp.zeros((width, rows), jnp.float32)
+        if t < slots - 1:
+            share_out(t + 1)
+            dq = lax.fori_loop(0, blocks, differentiate, dq, unroll=2)
+        else:
+            for step in range(slots):
+                j = far_first(step, slots)
+                dq = lax.fori_loop(
+                    0, group, lambda i, dq: differentiate(j * group + i, dq), dq, unroll=2
+                )
+                swap(j)
+                if step > 0:
+                    settle(far_first(step - 1, slots))
         dq_out[t] = (dq * scale).T.astype(jnp.bfloat16)
         move(*outward(0, t))
 
-    for t in range(slots):
-        work(t)
-
     factors = (scale, 1.0)
 
     def partial_sum(a, t, r):
-        other, place = peer(r)
         return remote(
             part_out.at[r - 1, a, t],
             part_in.at[r - 1, a, t],
             part_send.at[r - 1, a, t],
             part_recv.at[r - 1, a, t],
-            place,
+            peer(r)[1],
         )
 
-    for r in range(1, group):
-        for t in range(slots):
+    def swap(t):
+        for r in range(1, group):
             for a in range(2):
                 value = total[a, peer(r)[0] + group * t] * factors[a]
                 part_out[r - 1, a, t] = value.astype(jnp.bfloat16)
                 partial_sum(a, t, r).start()
-    for t in range(slots):
+
+    def settle(t):
         for a in range(2):
             value = total[a, share + group * t] * factors[a]
             for r in range(1, group):
@@ -243,6 +257,11 @@
                 value += part_in[r - 1, a, t].astype(jnp.float32)
             kv_out[a, t] = value.astype(jnp.bfloat16)
             move(*outward(a + 1, t))
+
+    share_out(0)
+    for t in range(slots):
+        work(t)
+    settle(far_first(slots - 1, slots))
 
     for a, ref in enumerate((dq_ref, dk_ref, dv_ref)):
         for h in range(heads):
@@ -259,6 +278,14 @@
                 partial_sum(a, t, r).wait_send()
 
 
+def hand_over(*refs):
+    copies = [pltpu.make_async_copy(refs[a], refs[a + 3], refs[6].at[a]) for a in range(3)]
+    for copy in copies:
+        copy.start()
+    for copy in copies:
+        copy.wait()
+
+
 def body(devices, batches, query_states, key_states, value_states, out_grad, head_offsets):
     rows, heads = query_states.shape[0], head_offsets.shape[0]
     width = query_states.shape[1] // heads
@@ -268,7 +295,7 @@
     anywhere = pl.BlockSpec(memory_space=pl.ANY)
     dma = pltpu.SemaphoreType.DMA
     result = jax.ShapeDtypeStruct(query_states.shape, half)
-    return pl.pallas_call(
+    landed = pl.pallas_call(
         functools.partial(kernel, devices, batches, heads),
         out_shape=(result,) * 3,
         in_specs=[pl.BlockSpec(memory_space=pltpu.SMEM)] + [anywhere] * 4,
@@ -278,6 +305,7 @@
             pltpu.VMEM((2, slots, rows, width), half),
             pltpu.VMEM((devices, rows, rows), full),
             pltpu.VMEM((devices, rows, rows), full),
+            pltpu.VMEM((devices, 1, rows), full),
             pltpu.VMEM((rows, rows), full),
             pltpu.VMEM((2, devices, rows, width), full),
             pltpu.VMEM((slots, rows, width), half),
@@ -297,6 +325,13 @@
             collective_id=0, has_side_effects=True, vmem_limit_bytes=56 * 2**20
         ),
     )(head_offsets, key_states, value_states, query_states, out_grad)
+    return pl.pallas_call(
+        hand_over,
+        out_shape=(result,) * 3,
+        in_specs=[anywhere] * 3,
+        out_specs=(anywhere,) * 3,
+        scratch_shapes=[dma((3,))],
+    )(*landed)
 
 
 def solution(mesh):

time: 57.5 us -> 75.6 us (1.31)
  Pallas kernels: 52.6 us -> 74 us
  local copies, waits for them, and re-layouts: 3.46 us -> 0 us
    pallas_call x0 -> x1, Pallas kernels: none -> 25 us  [body(): pl.pallas_call(hand_over, out_shape=(result,) * 3, in_specs=[anywhere] *...]
    pallas_call x1, Pallas kernels: 52.6 us -> 49 us  [body(): pl.pallas_call(functools.partial(kernel, devices, batches, heads), out_sh...]
    unnamed x7 -> x0, local copies, waits for them, and re-layouts: 3.46 us -> none
where the time goes in v2:
time: 75.6 us; the launch traced here: 74.6 us
  Pallas kernels  74 us (98%)
    pallas_call x1, Pallas kernels, body(): pl.pallas_call(functools.partial(kernel, devices, batches, heads), out_sh...  49 us
    pallas_call x1, Pallas kernels, body(): pl.pallas_call(hand_over, out_shape=(result,) * 3, in_specs=[anywhere] *...  25 us

profile of v2, /device:TPU:0, one launch (start us, length us, event | category | flops | bytes accessed | tf_op | source)
XLA Modules:
  0.0 74.6 jit_solution(3684910694415241117)
XLA Ops:
  0.6 49.0 %shard_map.76 = (bf16[256,512]{1,0:T(8,128)(2,1)}, bf16[256,512]{1,0:T(8,128)(2,1)}, bf16[256,512]{1,0:T(8,128)(2,1)}) custom-call(s32[4]{0:T(128)} %off_ref.1, bf16[256,512]{1,0:T(8,128)(2,1)} %key_ref.1, bf16[256,512]{1,0:T(8,128)(2,1)} %value_ref.1, bf16[256,512]{1,0:T(8,128)(2,1)} %query_ref.1, bf16[256,512]{1,0:T(8,128)(2,1)} %grad_ref.1), custom_call_target="tpu_custom_call" | custom-call | tf_op jit(solution)/shard_map/pallas_call | solution.py:298
  49.7 25.0 %shard_map.77 = (bf16[256,512]{1,0:T(8,128)(2,1)}, bf16[256,512]{1,0:T(8,128)(2,1)}, bf16[256,512]{1,0:T(8,128)(2,1)}) custom-call(bf16[256,512]{1,0:T(8,128)(2,1)} %get-tuple-element.6.refs_0_, bf16[256,512]{1,0:T(8,128)(2,1)} %get-tuple-element.7.refs_1_, bf16[256,512]{1,0:T(8,128)(2,1)} %get-tuple-element.8.refs_2_), custom_call_target="tpu_custom_call" | custom-call | tf_op jit(solution)/shard_map/pallas_call | solution.py:328

commit v3 on v2

--- a/solution.py
+++ b/solution.py
@@ -279,11 +279,8 @@
 
 
 def hand_over(*refs):
-    copies = [pltpu.make_async_copy(refs[a], refs[a + 3], refs[6].at[a]) for a in range(3)]
-    for copy in copies:
-        copy.start()
-    for copy in copies:
-        copy.wait()
+    for source, target in zip(refs[:3], refs[3:]):
+        target[...] = source[...]
 
 
 def body(devices, batches, query_states, key_states, value_states, out_grad, head_offsets):
@@ -325,13 +322,7 @@
             collective_id=0, has_side_effects=True, vmem_limit_bytes=56 * 2**20
         ),
     )(head_offsets, key_states, value_states, query_states, out_grad)
-    return pl.pallas_call(
-        hand_over,
-        out_shape=(result,) * 3,
-        in_specs=[anywhere] * 3,
-        out_specs=(anywhere,) * 3,
-        scratch_shapes=[dma((3,))],
-    )(*landed)
+    return pl.pallas_call(hand_over, out_shape=(result,) * 3)(*landed)
 
 
 def solution(mesh):

time: 75.6 us -> 52.7 us (0.70)
  Pallas kernels: 74 us -> 51 us
    pallas_call x1, Pallas kernels: 25 us -> 2 us  [body(): return pl.pallas_call(hand_over, out_shape=(result,) * 3)(*landed)]
where the time goes in v3:
time: 52.7 us; the launch traced here: 51.7 us
  Pallas kernels  51 us (97%)
  between operations  0.64 us (1%)
    pallas_call x1, Pallas kernels, body(): pl.pallas_call(functools.partial(kernel, devices, batches, heads), out_sh...  49 us
    pallas_call x1, Pallas kernels, body(): return pl.pallas_call(hand_over, out_shape=(result,) * 3)(*landed)  2 us

profile of v3, /device:TPU:0, one launch (start us, length us, event | category | flops | bytes accessed | tf_op | source)
XLA Modules:
  0.0 51.7 jit_solution(3792045378246330730)
XLA Ops:
  0.6 49.0 %shard_map.76 = (bf16[256,512]{1,0:T(8,128)(2,1)}, bf16[256,512]{1,0:T(8,128)(2,1)}, bf16[256,512]{1,0:T(8,128)(2,1)}) custom-call(s32[4]{0:T(128)} %off_ref.1, bf16[256,512]{1,0:T(8,128)(2,1)} %key_ref.1, bf16[256,512]{1,0:T(8,128)(2,1)} %value_ref.1, bf16[256,512]{1,0:T(8,128)(2,1)} %query_ref.1, bf16[256,512]{1,0:T(8,128)(2,1)} %grad_ref.1), custom_call_target="tpu_custom_call" | custom-call | tf_op jit(solution)/shard_map/pallas_call | solution.py:295
  49.7 2.0 %shard_map.77 = (bf16[256,512]{1,0:T(8,128)(2,1)}, bf16[256,512]{1,0:T(8,128)(2,1)}, bf16[256,512]{1,0:T(8,128)(2,1)}) custom-call(bf16[256,512]{1,0:T(8,128)(2,1)} %get-tuple-element.6.refs_0_, bf16[256,512]{1,0:T(8,128)(2,1)} %get-tuple-element.7.refs_1_, bf16[256,512]{1,0:T(8,128)(2,1)} %get-tuple-element.8.refs_2_), custom_call_target="tpu_custom_call" | custom-call | tf_op jit(solution)/shard_map/pallas_call | solution.py:325

commit v4 on v3

--- a/solution.py
+++ b/solution.py
@@ -32,8 +32,9 @@
     kv,
     qg,
     scores,
-    probs,
     tops,
+    stats,
+    dq_sum,
     level,
     total,
     dq_out,
@@ -123,7 +124,7 @@
             dst, recv = qg.at[a - 2, home_slot], qg_recv.at[a - 2, home_slot]
         return (src, dst, in_send.at[a, h], recv) + worker(h)
 
-    upward = head * 2 < heads
+    upward = home_slot * 2 < slots
 
     def far_first(step, count):
         return jnp.where(upward, count - 1 - step, step)
@@ -148,34 +149,52 @@
 
     lax.fori_loop(0, devices, clear, 0)
 
+    for t in range(slots):
+        stats[t, 0] = jnp.full((1, rows), MASKED, jnp.float32)
+        stats[t, 1] = jnp.zeros((1, rows), jnp.float32)
+        stats[t, 2] = jnp.zeros((1, rows), jnp.float32)
+        dq_sum[t] = jnp.zeros((width, rows), jnp.float32)
+
+    def near_first(step):
+        chosen = jnp.int32(0)
+        for base in range(slots):
+            nearest = sorted(range(slots), key=lambda t: abs(t - base))
+            chosen = jnp.where(home_slot == base, nearest[step], chosen)
+        return chosen
+
     def shared(a, t, r):
         slab = share + group * t
         block = kv.at[a, slab]
         return remote(block, block, peer_send.at[r - 1, a, t], kv_recv.at[a, slab], peer(r)[1])
 
-    def share_out(t):
+    def arrive(t):
         for a in range(2):
             slab = share + group * t
             landed(kv.at[a, slab], kv_recv.at[a, slab])
             for r in range(1, group):
                 shared(a, t, r).start()
+        for a in range(2):
+            landed(qg.at[a, t], qg_recv.at[a, t])
+        for a in range(2):
+            for r in range(1, group):
+                other = peer(r)[0] + group * t
+                landed(kv.at[a, other], kv_recv.at[a, other])
 
     def outward(a, t):
         src = dq_out.at[t] if a == 0 else kv_out.at[a - 1, t]
         dst = (dq_ref, dk_ref, dv_ref)[a].at[:, pl.ds(pl.multiple_of(head * width, width), width)]
         return (src, dst, out_send.at[a, t], out_recv.at[a, head]) + owner(t)
 
-    def work(t):
-        slab = share + group * t
-        for a in range(2):
-            for r in range(1, group):
-                other = peer(r)[0] + group * t
-                landed(kv.at[a, other], kv_recv.at[a, other])
-            landed(qg.at[a, t], qg_recv.at[a, t])
-        query, grad = qg[0, t], qg[1, t]
-
-        def score(j, carry):
+    def entry(query_slot, j):
+        return group * ((query_slot * (query_slot + 1)) >> 1) + j
+
+    def score_pair(query_slot, key_slot):
+        slab = share + group * query_slot
+        query, grad = qg[0, query_slot], qg[1, query_slot]
+
+        def score(i, carry):
             row_max, row_sum, row_dot = carry
+            j = key_slot * group + i
             s = contract(kv[0, j], query, 1, 1) * scale
             grad_probs = contract(kv[1, j], grad, 1, 1)
             ahead = (slab - j) * rows
@@ -194,41 +213,38 @@
             top = jnp.maximum(row_max, jnp.max(s, axis=0, keepdims=True))
             fade = jnp.exp(row_max - top)
             e = count * jnp.exp(s - top)
-            scores[j] = e
-            probs[j] = grad_probs
-            tops[j] = top
+            scores[entry(query_slot, j)] = e
+            tops[entry(query_slot, j)] = top
             row_sum = row_sum * fade + jnp.sum(e, axis=0, keepdims=True)
             row_dot = row_dot * fade + jnp.sum(e * grad_probs, axis=0, keepdims=True)
             return top, row_sum, row_dot
 
-        blocks = group * (t + 1)
-        zero = jnp.zeros((1, rows), jnp.float32)
-        start = (jnp.full((1, rows), MASKED, jnp.float32), zero, zero)
-        row_max, row_sum, row_dot = lax.fori_loop(0, blocks, score, start, unroll=2)
-        inverse = 1.0 / row_sum
-        grad_dot = row_dot * inverse
-
-        def differentiate(j, dq):
-            p = scores[j] * (jnp.exp(tops[j] - row_max) * inverse)
-            ds = (p * (probs[j] - grad_dot)).astype(jnp.bfloat16)
+        carry = tuple(stats[query_slot, n] for n in range(3))
+        carry = lax.fori_loop(0, group, score, carry, unroll=2)
+        for n in range(3):
+            stats[query_slot, n] = carry[n]
+
+    def differentiate(query_slot, key_slot):
+        query, grad = qg[0, query_slot], qg[1, query_slot]
+        row_max = stats[query_slot, 0]
+        inverse = 1.0 / stats[query_slot, 1]
+        grad_dot = stats[query_slot, 2] * inverse
+
+        def block(i, dq):
+            j = key_slot * group + i
+            at = entry(query_slot, j)
+            p = scores[at] * (jnp.exp(tops[at] - row_max) * inverse)
+            grad_probs = contract(kv[1, j], grad, 1, 1)
+            ds = (p * (grad_probs - grad_dot)).astype(jnp.bfloat16)
             total[1, j] += contract(p.astype(jnp.bfloat16), grad, 1, 0)
             total[0, j] += contract(ds, query, 1, 0)
             return dq + contract(kv[0, j], ds, 0, 0)
 
         dq = jnp.zeros((width, rows), jnp.float32)
-        if t < slots - 1:
-            share_out(t + 1)
-            dq = lax.fori_loop(0, blocks, differentiate, dq, unroll=2)
-        else:
-            for step in range(slots):
-                j = far_first(step, slots)
-                dq = lax.fori_loop(
-                    0, group, lambda i, dq: differentiate(j * group + i, dq), dq, unroll=2
-                )
-                swap(j)
-                if step > 0:
-                    settle(far_first(step - 1, slots))
-        dq_out[t] = (dq * scale).T.astype(jnp.bfloat16)
+        dq_sum[query_slot] += lax.fori_loop(0, group, block, dq, unroll=2)
+
+    def finish_query(t):
+        dq_out[t] = (dq_sum[t] * scale).T.astype(jnp.bfloat16)
         move(*outward(0, t))
 
     factors = (scale, 1.0)
@@ -258,9 +274,34 @@
             kv_out[a, t] = value.astype(jnp.bfloat16)
             move(*outward(a + 1, t))
 
-    share_out(0)
-    for t in range(slots):
-        work(t)
+    order = [near_first(step) for step in range(slots)]
+    for step in range(slots):
+        arrive(order[step])
+        for other in order[: step + 1]:
+            score_pair(jnp.maximum(order[step], other), jnp.minimum(order[step], other))
+
+    for step in range(slots):
+        key_slot = far_first(step, slots)
+
+        def one(query_slot, _):
+            differentiate(query_slot, key_slot)
+            return 0
+
+        lax.fori_loop(key_slot, slots, one, 0)
+        swap(key_slot)
+
+        @pl.when(jnp.logical_not(upward))
+        def _():
+            finish_query(key_slot)
+
+        if step > 0:
+            settle(far_first(step - 1, slots))
+
+    @pl.when(upward)
+    def _():
+        for t in reversed(range(slots)):
+            finish_query(t)
+
     settle(far_first(slots - 1, slots))
 
     for a, ref in enumerate((dq_ref, dk_ref, dv_ref)):
@@ -288,6 +329,7 @@
     width = query_states.shape[1] // heads
     group = devices // heads
     slots = devices // group
+    entries = group * (slots * (slots + 1) // 2)
     half, full = jnp.bfloat16, jnp.float32
     anywhere = pl.BlockSpec(memory_space=pl.ANY)
     dma = pltpu.SemaphoreType.DMA
@@ -300,9 +342,10 @@
         scratch_shapes=[
             pltpu.VMEM((2, devices, rows, width), half),
             pltpu.VMEM((2, slots, rows, width), half),
-            pltpu.VMEM((devices, rows, rows), full),
-            pltpu.VMEM((devices, rows, rows), full),
-            pltpu.VMEM((devices, 1, rows), full),
+            pltpu.VMEM((entries, rows, rows), full),
+            pltpu.VMEM((entries, 1, rows), full),
+            pltpu.VMEM((slots, 3, 1, rows), full),
+            pltpu.VMEM((slots, width, rows), full),
             pltpu.VMEM((rows, rows), full),
             pltpu.VMEM((2, devices, rows, width), full),
             pltpu.VMEM((slots, rows, width), half),

time: 52.7 us -> 53.7 us (1.019)
  Pallas kernels: 51 us -> 52.1 us
    pallas_call x1, Pallas kernels: 49 us -> 50.1 us  [body(): pl.pallas_call(functools.partial(kernel, devices, batches, heads), out_sh...]
where the time goes in v4:
time: 53.7 us; the launch traced here: 52.7 us
  Pallas kernels  52.1 us (97%)
  between operations  0.64 us (1%)
    pallas_call x1, Pallas kernels, body(): pl.pallas_call(functools.partial(kernel, devices, batches, heads), out_sh...  50.1 us
    pallas_call x1, Pallas kernels, body(): return pl.pallas_call(hand_over, out_shape=(result,) * 3)(*landed)  2 us

profile of v4, /device:TPU:0, one launch (start us, length us, event | category | flops | bytes accessed | tf_op | source)
XLA Modules:
  0.0 52.7 jit_solution(5093770759981333176)
XLA Ops:
  0.6 50.1 %shard_map.76 = (bf16[256,512]{1,0:T(8,128)(2,1)}, bf16[256,512]{1,0:T(8,128)(2,1)}, bf16[256,512]{1,0:T(8,128)(2,1)}) custom-call(s32[4]{0:T(128)} %off_ref.1, bf16[256,512]{1,0:T(8,128)(2,1)} %key_ref.1, bf16[256,512]{1,0:T(8,128)(2,1)} %value_ref.1, bf16[256,512]{1,0:T(8,128)(2,1)} %query_ref.1, bf16[256,512]{1,0:T(8,128)(2,1)} %grad_ref.1), custom_call_target="tpu_custom_call" | custom-call | tf_op jit(solution)/shard_map/pallas_call | solution.py:337
  50.7 2.0 %shard_map.77 = (bf16[256,512]{1,0:T(8,128)(2,1)}, bf16[256,512]{1,0:T(8,128)(2,1)}, bf16[256,512]{1,0:T(8,128)(2,1)}) custom-call(bf16[256,512]{1,0:T(8,128)(2,1)} %get-tuple-element.6.refs_0_, bf16[256,512]{1,0:T(8,128)(2,1)} %get-tuple-element.7.refs_1_, bf16[256,512]{1,0:T(8,128)(2,1)} %get-tuple-element.8.refs_2_), custom_call_target="tpu_custom_call" | custom-call | tf_op jit(solution)/shard_map/pallas_call | solution.py:368

commit v5 on v4

--- a/solution.py
+++ b/solution.py
@@ -15,6 +15,22 @@
     return lax.dot_general(
         left, right, (((left_dim,), (right_dim,)), ((), ())), preferred_element_type=jnp.float32
     )
+
+
+def send_order(count, base):
+    upper = base * 2 >= count
+    same = [t for t in range(count) if (t * 2 >= count) == upper and t != base]
+    cross = [t for t in range(count) if (t * 2 >= count) != upper]
+    cross = sorted(cross, key=lambda t: -abs(t - base))
+    inner = abs(2 * base + 1 - count) * 2 < count
+    return [base] + (same + cross if inner else cross + same)
+
+
+def arrival_order(count, base):
+    def key(t):
+        return send_order(count, t).index(base), abs(t - base)
+
+    return sorted(range(count), key=key)
 
 
 def kernel(
@@ -124,6 +140,12 @@
             dst, recv = qg.at[a - 2, home_slot], qg_recv.at[a - 2, home_slot]
         return (src, dst, in_send.at[a, h], recv) + worker(h)
 
+    def ordered(order, count, step):
+        chosen = jnp.int32(0)
+        for base in range(count):
+            chosen = jnp.where(home_slot == base, order(count, base)[step], chosen)
+        return chosen
+
     upward = home_slot * 2 < slots
 
     def far_first(step, count):
@@ -131,7 +153,7 @@
 
     for step in range(heads):
         for a in range(4):
-            move(*inward(a, far_first(step, heads)))
+            move(*inward(a, ordered(send_order, heads, step)))
 
     offset = off_ref[head]
     key_row = lax.broadcasted_iota(jnp.int32, (rows, rows), 0)
@@ -154,13 +176,6 @@
         stats[t, 1] = jnp.zeros((1, rows), jnp.float32)
         stats[t, 2] = jnp.zeros((1, rows), jnp.float32)
         dq_sum[t] = jnp.zeros((width, rows), jnp.float32)
-
-    def near_first(step):
-        chosen = jnp.int32(0)
-        for base in range(slots):
-            nearest = sorted(range(slots), key=lambda t: abs(t - base))
-            chosen = jnp.where(home_slot == base, nearest[step], chosen)
-        return chosen
 
     def shared(a, t, r):
         slab = share + group * t
@@ -274,7 +289,7 @@
             kv_out[a, t] = value.astype(jnp.bfloat16)
             move(*outward(a + 1, t))
 
-    order = [near_first(step) for step in range(slots)]
+    order = [ordered(arrival_order, slots, step) for step in range(slots)]
     for step in range(slots):
         arrive(order[step])
         for other in order[: step + 1]:

time: 53.7 us -> 54 us (level)
  the two profiles are of different devices: /device:TPU:0 before, /device:TPU:9 now
where the time goes in v5:
time: 54 us; the launch traced here: 53.8 us
  Pallas kernels  53.2 us (99%)
  between operations  0.64 us (1%)
    pallas_call x1, Pallas kernels, body(): pl.pallas_call(functools.partial(kernel, devices, batches, heads), out_sh...  51.2 us
    pallas_call x1, Pallas kernels, body(): return pl.pallas_call(hand_over, out_shape=(result,) * 3)(*landed)  2 us

profile of v5, /device:TPU:9, one launch (start us, length us, event | category | flops | bytes accessed | tf_op | source)
XLA Modules:
  0.0 53.8 jit_solution(12565306315753897994)
XLA Ops:
  0.6 51.2 %shard_map.76 = (bf16[256,512]{1,0:T(8,128)(2,1)}, bf16[256,512]{1,0:T(8,128)(2,1)}, bf16[256,512]{1,0:T(8,128)(2,1)}) custom-call(s32[4]{0:T(128)} %off_ref.1, bf16[256,512]{1,0:T(8,128)(2,1)} %key_ref.1, bf16[256,512]{1,0:T(8,128)(2,1)} %value_ref.1, bf16[256,512]{1,0:T(8,128)(2,1)} %query_ref.1, bf16[256,512]{1,0:T(8,128)(2,1)} %grad_ref.1), custom_call_target="tpu_custom_call" | custom-call | tf_op jit(solution)/shard_map/pallas_call | solution.py:352
  51.8 2.0 %shard_map.77 = (bf16[256,512]{1,0:T(8,128)(2,1)}, bf16[256,512]{1,0:T(8,128)(2,1)}, bf16[256,512]{1,0:T(8,128)(2,1)}) custom-call(bf16[256,512]{1,0:T(8,128)(2,1)} %get-tuple-element.6.refs_0_, bf16[256,512]{1,0:T(8,128)(2,1)} %get-tuple-element.7.refs_1_, bf16[256,512]{1,0:T(8,128)(2,1)} %get-tuple-element.8.refs_2_), custom_call_target="tpu_custom_call" | custom-call | tf_op jit(solution)/shard_map/pallas_call | solution.py:383

commit v6 on v3

--- a/solution.py
+++ b/solution.py
@@ -174,7 +174,10 @@
             landed(qg.at[a, t], qg_recv.at[a, t])
         query, grad = qg[0, t], qg[1, t]
 
-        def score(j, carry):
+        def score(key_slot, i, carry):
+            j = key_slot * group + i
+            closest = group * (t - key_slot) - (group - 1)
+            farthest = group * (t - key_slot) + (group - 1)
             row_max, row_sum, row_dot = carry
             s = contract(kv[0, j], query, 1, 1) * scale
             grad_probs = contract(kv[1, j], grad, 1, 1)
@@ -187,10 +190,16 @@
                 - lax.broadcasted_iota(jnp.int32, (rows, rows), 0)
                 + ahead
             )
-            near = jnp.where(distance < WINDOW, 1.0, 0.0)
-            count = near + jnp.maximum(level[...] - higher.astype(jnp.float32), 0.0)
-            count = jnp.where(distance >= 0, count, 0.0)
-            s = jnp.where(count > 0.0, s, MASKED)
+            count = jnp.maximum(level[...] - higher.astype(jnp.float32), 0.0)
+            inside = (farthest + 1) * rows - 1 < WINDOW
+            if inside:
+                count += 1.0
+            elif (closest - 1) * rows + 1 < WINDOW:
+                count += jnp.where(distance < WINDOW, 1.0, 0.0)
+            if closest < 1:
+                count = jnp.where(distance >= 0, count, 0.0)
+            if not inside or closest < 1:
+                s = jnp.where(count > 0.0, s, MASKED)
             top = jnp.maximum(row_max, jnp.max(s, axis=0, keepdims=True))
             fade = jnp.exp(row_max - top)
             e = count * jnp.exp(s - top)
@@ -201,10 +210,11 @@
             row_dot = row_dot * fade + jnp.sum(e * grad_probs, axis=0, keepdims=True)
             return top, row_sum, row_dot
 
-        blocks = group * (t + 1)
         zero = jnp.zeros((1, rows), jnp.float32)
         start = (jnp.full((1, rows), MASKED, jnp.float32), zero, zero)
-        row_max, row_sum, row_dot = lax.fori_loop(0, blocks, score, start, unroll=2)
+        for key_slot in range(t + 1):
+            start = lax.fori_loop(0, group, functools.partial(score, key_slot), start, unroll=2)
+        row_max, row_sum, row_dot = start
         inverse = 1.0 / row_sum
         grad_dot = row_dot * inverse
 
@@ -218,7 +228,10 @@
         dq = jnp.zeros((width, rows), jnp.float32)
         if t < slots - 1:
             share_out(t + 1)
-            dq = lax.fori_loop(0, blocks, differentiate, dq, unroll=2)
+            for key_slot in range(t + 1):
+                dq = lax.fori_loop(
+                    key_slot * group, (key_slot + 1) * group, differentiate, dq, unroll=2
+                )
         else:
             for step in range(slots):
                 j = far_first(step, slots)

time: 52.7 us -> 51.4 us (0.975); the launches traced: 51.7 us -> 51 us
  Pallas kernels: 51 us -> 50.3 us
    pallas_call x1, Pallas kernels: 49 us -> 48.3 us  [body(): pl.pallas_call(functools.partial(kernel, devices, batches, heads), out_sh...]
where the time goes in v6:
time: 51.4 us; the launch traced here: 51 us
  Pallas kernels  50.3 us (98%)
  between operations  0.64 us (1%)
    pallas_call x1, Pallas kernels, body(): pl.pallas_call(functools.partial(kernel, devices, batches, heads), out_sh...  48.3 us
    pallas_call x1, Pallas kernels, body(): return pl.pallas_call(hand_over, out_shape=(result,) * 3)(*landed)  2 us

profile of v6, /device:TPU:0, one launch (start us, length us, event | category | flops | bytes accessed | tf_op | source)
XLA Modules:
  0.0 51.0 jit_solution(12791544840937755113)
XLA Ops:
  0.6 48.3 %shard_map.76 = (bf16[256,512]{1,0:T(8,128)(2,1)}, bf16[256,512]{1,0:T(8,128)(2,1)}, bf16[256,512]{1,0:T(8,128)(2,1)}) custom-call(s32[4]{0:T(128)} %off_ref.1, bf16[256,512]{1,0:T(8,128)(2,1)} %key_ref.1, bf16[256,512]{1,0:T(8,128)(2,1)} %value_ref.1, bf16[256,512]{1,0:T(8,128)(2,1)} %query_ref.1, bf16[256,512]{1,0:T(8,128)(2,1)} %grad_ref.1), custom_call_target="tpu_custom_call" | custom-call | tf_op jit(solution)/shard_map/pallas_call | solution.py:308
  49.0 2.0 %shard_map.77 = (bf16[256,512]{1,0:T(8,128)(2,1)}, bf16[256,512]{1,0:T(8,128)(2,1)}, bf16[256,512]{1,0:T(8,128)(2,1)}) custom-call(bf16[256,512]{1,0:T(8,128)(2,1)} %get-tuple-element.6.refs_0_, bf16[256,512]{1,0:T(8,128)(2,1)} %get-tuple-element.7.refs_1_, bf16[256,512]{1,0:T(8,128)(2,1)} %get-tuple-element.8.refs_2_), custom_call_target="tpu_custom_call" | custom-call | tf_op jit(solution)/shard_map/pallas_call | solution.py:338

commit v7 on v6

--- a/solution.py
+++ b/solution.py
@@ -55,6 +55,7 @@
     slots = devices // group
     level_count = devices.bit_length() - 1
     scale = width ** (-0.5)
+    step_blocks = 2 if group % 2 == 0 else 1
 
     seq, batch = lax.axis_index("seq"), lax.axis_index("batch")
     unit = seq // spots
@@ -174,11 +175,9 @@
             landed(qg.at[a, t], qg_recv.at[a, t])
         query, grad = qg[0, t], qg[1, t]
 
-        def score(key_slot, i, carry):
-            j = key_slot * group + i
+        def masked(key_slot, j):
             closest = group * (t - key_slot) - (group - 1)
             farthest = group * (t - key_slot) + (group - 1)
-            row_max, row_sum, row_dot = carry
             s = contract(kv[0, j], query, 1, 1) * scale
             grad_probs = contract(kv[1, j], grad, 1, 1)
             ahead = (slab - j) * rows
@@ -200,20 +199,33 @@
                 count = jnp.where(distance >= 0, count, 0.0)
             if not inside or closest < 1:
                 s = jnp.where(count > 0.0, s, MASKED)
-            top = jnp.maximum(row_max, jnp.max(s, axis=0, keepdims=True))
+            probs[j] = grad_probs
+            return s, count, grad_probs
+
+        def score(key_slot, i, carry):
+            row_max, row_sum, row_dot = carry
+            first = key_slot * group + i * step_blocks
+            parts = [masked(key_slot, first + n) for n in range(step_blocks)]
+            highest = functools.reduce(jnp.maximum, [part[0] for part in parts])
+            top = jnp.maximum(row_max, jnp.max(highest, axis=0, keepdims=True))
             fade = jnp.exp(row_max - top)
-            e = count * jnp.exp(s - top)
-            scores[j] = e
-            probs[j] = grad_probs
-            tops[j] = top
-            row_sum = row_sum * fade + jnp.sum(e, axis=0, keepdims=True)
-            row_dot = row_dot * fade + jnp.sum(e * grad_probs, axis=0, keepdims=True)
+            weights, dots = 0.0, 0.0
+            for n, (s, count, grad_probs) in enumerate(parts):
+                e = count * jnp.exp(s - top)
+                scores[first + n] = e
+                tops[first + n] = top
+                weights += e
+                dots += e * grad_probs
+            row_sum = row_sum * fade + jnp.sum(weights, axis=0, keepdims=True)
+            row_dot = row_dot * fade + jnp.sum(dots, axis=0, keepdims=True)
             return top, row_sum, row_dot
 
         zero = jnp.zeros((1, rows), jnp.float32)
         start = (jnp.full((1, rows), MASKED, jnp.float32), zero, zero)
         for key_slot in range(t + 1):
-            start = lax.fori_loop(0, group, functools.partial(score, key_slot), start, unroll=2)
+            start = lax.fori_loop(
+                0, group // step_blocks, functools.partial(score, key_slot), start
+            )
         row_max, row_sum, row_dot = start
         inverse = 1.0 / row_sum
         grad_dot = row_dot * inverse

time: 51.4 us -> 51.5 us (level)
  no operation moved by 1% of the time
where the time goes in v7:
time: 51.5 us; the launch traced here: 51 us
  Pallas kernels  50.3 us (98%)
  between operations  0.64 us (1%)
    pallas_call x1, Pallas kernels, body(): pl.pallas_call(functools.partial(kernel, devices, batches, heads), out_sh...  48.3 us
    pallas_call x1, Pallas kernels, body(): return pl.pallas_call(hand_over, out_shape=(result,) * 3)(*landed)  2 us

profile of v7, /device:TPU:0, one launch (start us, length us, event | category | flops | bytes accessed | tf_op | source)
XLA Modules:
  0.0 51.0 jit_solution(6093996824595807091)
XLA Ops:
  0.6 48.3 %shard_map.76 = (bf16[256,512]{1,0:T(8,128)(2,1)}, bf16[256,512]{1,0:T(8,128)(2,1)}, bf16[256,512]{1,0:T(8,128)(2,1)}) custom-call(s32[4]{0:T(128)} %off_ref.1, bf16[256,512]{1,0:T(8,128)(2,1)} %key_ref.1, bf16[256,512]{1,0:T(8,128)(2,1)} %value_ref.1, bf16[256,512]{1,0:T(8,128)(2,1)} %query_ref.1, bf16[256,512]{1,0:T(8,128)(2,1)} %grad_ref.1), custom_call_target="tpu_custom_call" | custom-call | tf_op jit(solution)/shard_map/pallas_call | solution.py:320
  49.0 2.0 %shard_map.77 = (bf16[256,512]{1,0:T(8,128)(2,1)}, bf16[256,512]{1,0:T(8,128)(2,1)}, bf16[256,512]{1,0:T(8,128)(2,1)}) custom-call(bf16[256,512]{1,0:T(8,128)(2,1)} %get-tuple-element.6.refs_0_, bf16[256,512]{1,0:T(8,128)(2,1)} %get-tuple-element.7.refs_1_, bf16[256,512]{1,0:T(8,128)(2,1)} %get-tuple-element.8.refs_2_), custom_call_target="tpu_custom_call" | custom-call | tf_op jit(solution)/shard_map/pallas_call | solution.py:350
